TPU v7x, 256 devices: a whole 4x4x8 slice. The times are simulated.
256 devices in a mesh: pairs: 32 (over z, x), side: 2 (over core), mp: 4 (over y).
Axes of the slice: x: 4, y: 4, z: 8, core: 2. Of those that a mesh axis runs over, the one named last changes fastest.
Arguments:
- enc_tokens: bfloat16 [256, 512, 1024], P('pairs', 'mp'), may hold values from -6 to 6
- pair_views: int32 [128, 2], replicated, may hold values from 0 to 255, as said below
- embed_weight: bfloat16 [1024, 768], replicated, may hold values from -0.1875 to 0.1875
- self_qkv: bfloat16 [2, 3, 768, 768], P('side', None, None, 'mp'), may hold values from -10 to 10
- self_out: bfloat16 [2, 768, 768], P('side'), may hold values from -0.21875 to 0.21875
- cross_query: bfloat16 [2, 768, 768], P('side', None, 'mp'), may hold values from -1 to 1
- cross_kv: bfloat16 [2, 2, 768, 768], P('side', None, None, 'mp'), may hold values from -10 to 10
- cross_out: bfloat16 [2, 768, 768], P('side'), may hold values from -0.21875 to 0.21875
- norm_gains: float32 [2, 4, 768], P('side'), may hold values from 0.25 to 1.75
- head_weight: bfloat16 [2, 768, 1024], P('side'), may hold values from -0.21875 to 0.21875
Outputs:
- pointmaps: bfloat16 [128, 2, 512, 1024], P('pairs', 'side', 'mp')
Inputs may be any that keep to these rules, and one draw needn't show every extreme that they name: `pair_views`: the two ids of a pair lie in different blocks of 8 consecutive ids. For each block of 4 consecutive pairs and each side, at most 1 of its ids lie in any one block of 8 consecutive ids, and some block holds exactly 1.
All inputs are finite; a program needn't handle non-finite values.
Results may differ from a plain program's by a relative error of at most 0.023.
Values may be sent and summed in bfloat16 or wider, within the bound.
No kernel may reach another device: no remote copies, remote signals or barrier semaphores. Data moves between devices by JAX's collectives and lax.ppermute only.
A program may use at most 128 MiB of HBM per device.

v0:
```python
import jax
import jax.numpy as jnp
from jax import lax
from jax.sharding import PartitionSpec as P

D = 768
HEADS = 12


def swapped(value, axis, apart):
    mask = 2**apart
    pairs = [(source, source ^ mask) for source in range(lax.axis_size(axis))]
    return lax.ppermute(value, axis, pairs)


def layer_norm(values, gain):
    average = jnp.mean(values, axis=-1, keepdims=True)
    centred = values - average
    spread = jnp.mean(centred * centred, axis=-1, keepdims=True)
    return centred * lax.rsqrt(spread + 1e-06) * gain


def attend_heads(queries, key_rows, value_rows):
    pair_count, token_count, columns = queries.shape
    head_dim = D // HEADS
    shaped = (pair_count, token_count, columns // head_dim, head_dim)
    scores = jnp.einsum(
        "pqhd,pkhd->phqk",
        queries.reshape(shaped),
        key_rows.reshape(shaped),
        preferred_element_type=jnp.float32,
    ) * head_dim ** (-0.5)
    weights = jax.nn.softmax(scores, axis=-1).astype(jnp.bfloat16)
    mixture = jnp.einsum(
        "phqk,pkhd->pqhd", weights, value_rows.reshape(shaped), preferred_element_type=jnp.float32
    )
    return mixture.reshape(pair_count, token_count, columns).astype(jnp.bfloat16)


def collect(row_block, weight):
    return jnp.einsum(
        "prd,cde->prce",
        lax.all_gather(row_block, "mp", axis=1, tiled=True),
        weight,
        preferred_element_type=jnp.float32,
    ).astype(jnp.bfloat16)


def to_rows(attended, weight):
    return jnp.einsum(
        "prd,de->pre",
        lax.all_to_all(attended, "mp", split_axis=1, concat_axis=2, tiled=True),
        weight,
        preferred_element_type=jnp.float32,
    )


def partner_of(row_block):
    return swapped(row_block, "side", 0)


def local(
    enc_tokens,
    pair_views,
    embed_weight,
    self_qkv,
    self_out,
    cross_query,
    cross_kv,
    cross_out,
    norm_gains,
    head_weight,
):
    owner_count = lax.axis_size("pairs")
    own_index = lax.axis_index("pairs")
    side_index = lax.axis_index("side")
    view_dev, row_count, enc_width = enc_tokens.shape
    pair_dev = pair_views.shape[0] // owner_count
    capacity = (pair_dev + owner_count - 1) // owner_count
    wanted = jnp.where(side_index == 0, pair_views[:, 0], pair_views[:, 1]).reshape(
        owner_count, pair_dev
    )
    holder = wanted // view_dev
    within = wanted % view_dev
    positions = jnp.arange(pair_dev)
    before = positions[None, :] < positions[:, None]
    slot_rank = jnp.sum((holder[:, :, None] == holder[:, None, :]) & before[None], axis=2)
    chosen = (holder == own_index)[:, None, :] & (
        slot_rank[:, None, :] == jnp.arange(capacity)[None, :, None]
    )
    source = jnp.sum(jnp.where(chosen, within[:, None, :], 0), axis=2).reshape(-1)
    filled = jnp.any(chosen, axis=2).reshape(-1)
    arrival = holder[own_index] * capacity + slot_rank[own_index]
    packet = jnp.where(filled[:, None, None], enc_tokens[source], jnp.zeros((), jnp.bfloat16))
    packet = packet.reshape(owner_count, capacity, row_count, enc_width)
    received = lax.all_to_all(packet, "pairs", split_axis=0, concat_axis=0, tiled=True)
    fetched = received.reshape(owner_count * capacity, row_count, enc_width)[arrival]
    own_rows = jnp.einsum(
        "pre,ed->prd", fetched, embed_weight, preferred_element_type=jnp.float32
    ).astype(jnp.bfloat16)
    gain_rows = norm_gains[0]
    normed = layer_norm(own_rows.astype(jnp.float32), gain_rows[0]).astype(jnp.bfloat16)
    projected = collect(normed, self_qkv[0])
    attended = attend_heads(projected[:, :, 0], projected[:, :, 1], projected[:, :, 2])
    after_self = own_rows.astype(jnp.float32) + to_rows(attended, self_out[0])
    partner_rows = partner_of(own_rows)
    partner_normed = layer_norm(partner_rows.astype(jnp.float32), gain_rows[2]).astype(jnp.bfloat16)
    partner_kv = collect(partner_normed, cross_kv[0])
    query_normed = layer_norm(after_self, gain_rows[1]).astype(jnp.bfloat16)
    cross_queries = collect(query_normed, cross_query)
    crossed = attend_heads(cross_queries[:, :, 0], partner_kv[:, :, 0], partner_kv[:, :, 1])
    after_cross = after_self + to_rows(crossed, cross_out[0])
    final_rows = layer_norm(after_cross, gain_rows[3]).astype(jnp.bfloat16)
    result = jnp.einsum(
        "prd,de->pre", final_rows, head_weight[0], preferred_element_type=jnp.float32
    )
    return result.astype(jnp.bfloat16)[:, None]


def solution(mesh):
    placed = (
        P("pairs", "mp", None),
        P(),
        P(),
        P("side", None, None, "mp"),
        P("side", None, None),
        P("side", None, "mp"),
        P("side", None, None, "mp"),
        P("side", None, None),
        P("side", None, None),
        P("side", None, None),
    )
    return jax.shard_map(
        local, mesh=mesh, in_specs=placed, out_specs=P("pairs", "side", "mp", None), check_vma=False
    )
```

profile of v0, /device:TPU:2, one launch (start us, length us, event | category | flops | bytes accessed | tf_op | source)
XLA Modules:
  0.0 427.6 jit_solution(13365358870764441674)
XLA Ops:
  6.5 0.5 broadcast.483
  7.1 1.5 fusion.73
  8.6 0.1 select_n.147
  8.7 0.1 copy.63
  8.8 0.1 convert_reduce_fusion.2
  8.9 0.1 copy.67
  9.0 0.1 select_n.145
  9.1 0.1 fusion.71
  9.2 0.1 fusion.61
  9.4 4.8 %gather_fusion = bf16[32,128,1024]{2,1,0:T(8,128)(2,1)} fusion(bf16[8,128,1024]{2,1,0:T(8,128)(2,1)S(1)} %copy-done, s32[1024]{0:T(1024)S(1)} %pad_clamp_fusion.1), kind=kCustom, calls=%fused_computation | custom fusion | bytes 16777344 | tf_op jit(solution)/shard_map/gather | solution.py:94
  14.2 7.2 %bitcast_select_fusion = bf16[32,1,128,1024]{3,2,1,0:T(8,128)(2,1)} fusion(bf16[32,128,1024]{2,1,0:T(8,128)(2,1)} %gather_fusion, pred[32]{0:T(512)(128)(4,1)S(1)} %get-tuple-element.9), kind=kLoop, calls=%fused_computation.12 | loop fusion | flops 4194304 | bytes 16777248 | tf_op jit(solution)/shard_map/jit(_where)/select_n | solution.py:94
  21.4 11.8 %all-to-all-start = ((bf16[32,1,128,1024]{3,2,1,0:T(8,128)(2,1)}), bf16[32,1,128,1024]{3,2,1,0:T(8,128)(2,1)}, u32[]{:S(2)}, u32[]{:S(2)}) async-start(bf16[32,1,128,1024]{3,2,1,0:T(8,128)(2,1)} %bitcast_select_fusion), calls=%async_computation | async-start | bytes 16777216 | tf_op jit(solution)/shard_map/all_to_all | solution.py:96
  33.2 0.0 all-gather.4.cloned.1.call-start
  33.3 0.2 add_reduce_fusion
  33.5 185.6 %all-to-all-done = bf16[32,1,128,1024]{3,2,1,0:T(8,128)(2,1)} async-done(((bf16[32,1,128,1024]{3,2,1,0:T(8,128)(2,1)}), bf16[32,1,128,1024]{3,2,1,0:T(8,128)(2,1)}, u32[]{:S(2)}, u32[]{:S(2)}) %all-to-all-start) | async-done | bytes 8388640 | tf_op jit(solution)/shard_map/all_to_all | solution.py:96
  219.1 4.0 gather_fusion.1
  223.1 2.5 convert_reduce_fusion
  225.6 0.4 fusion.30
  225.9 1.2 fusion.32
  227.2 0.1 collective-permute-start
  227.3 2.3 collective-permute-done
  229.6 0.2 convert_reduce_fusion.1
  229.8 0.4 fusion.33
  230.2 1.2 fusion.35
  231.5 41.8 %all-gather.4.cloned.1.call-done = bf16[4,512,768]{2,1,0:T(8,128)(2,1)} async-done(((bf16[4,128,768]{2,1,0:T(8,128)(2,1)}), bf16[4,512,768]{2,1,0:T(8,128)(2,1)}) %all-gather.4.cloned.1.call-update) | async-done | bytes 3145744 | tf_op jit(solution)/shard_map/all_gather | solution.py:43
  273.2 3.9 fusion.20
  277.1 1.2 fusion.74
  278.3 10.0 %fusion.76 = (f32[4,3,512]{2,1,0:T(4,128)S(1)}, f32[4,3,512,512]{2,3,1,0:T(8,128)}) fusion(bf16[4,512,3,64]{1,3,2,0:T(8,128)(2,1)} %bitcast.114, bf16[4,512,3,64]{1,3,2,0:T(8,128)(2,1)S(1)} %bitcast.113), kind=kOutput, calls=%fused_computation.111 | convolution fusion | flops 412090880 | bytes 14180352 | tf_op jit(solution)/shard_map/sub | solution.py:33
  288.3 6.0 %fusion.47 = bf16[4,3,64,512]{3,2,1,0:T(8,128)(2,1)S(1)} fusion(bf16[4,512,3,64]{1,3,2,0:T(8,128)(2,1)S(1)} %bitcast.112, f32[4,3,512,512]{2,3,1,0:T(8,128)} %get-tuple-element.21, f32[4,3,512]{2,1,0:T(4,128)S(1)} %get-tuple-element.20), kind=kOutput, calls=%fused_computation.52 | convolution fusion | flops 409337856 | bytes 14180352 | tf_op jit(solution)/shard_map/phqk,pkhd->pqhd/dot_general | solution.py:34
  294.4 0.7 copy.69
  295.1 30.3 %all_to_all.41 = bf16[4,512,192]{2,0,1:T(4,128)(2,1)S(1)} all-to-all(bf16[4,512,192]{2,0,1:T(4,128)(2,1)S(1)} %copy.69), channel_id=1, replica_groups=mesh['pairs'=32,'side'=2,'mp'=4] {'mp'}, dimensions={1} | all-to-all | bytes 1572864 | tf_op jit(solution)/shard_map/all_to_all | solution.py:52
  325.4 1.4 copy.71
  326.8 2.4 fusion.77
  329.2 0.3 multiply_reduce_fusion.3
  329.5 1.1 multiply_convert_fusion.1
  330.7 3.3 fusion.27
  334.1 1.0 fusion.75
  335.1 37.7 %all-gather.8.cloned.1.call-done = bf16[4,512,768]{2,1,0:T(8,128)(2,1)} async-done(((bf16[4,128,768]{2,1,0:T(8,128)(2,1)}), bf16[4,512,768]{2,1,0:T(8,128)(2,1)}) %all-gather.8.cloned.1.call-update) | async-done | bytes 3145744 | tf_op jit(solution)/shard_map/all_gather | solution.py:43
  372.8 4.0 convolution_convert_fusion
  376.7 10.1 %fusion.78 = (f32[4,3,512]{2,1,0:T(4,128)S(1)}, f32[4,3,512,512]{2,3,1,0:T(8,128)}) fusion(bf16[4,512,3,64]{1,3,2,0:T(8,128)(2,1)} %bitcast.120, bf16[4,512,3,64]{1,3,2,0:T(8,128)(2,1)} %bitcast.118), kind=kOutput, calls=%fused_computation.113 | convolution fusion | flops 412090880 | bytes 14180352 | tf_op jit(solution)/shard_map/sub | solution.py:33
  386.8 6.7 %fusion.46 = bf16[4,3,64,512]{3,2,1,0:T(8,128)(2,1)} fusion(bf16[4,512,3,64]{1,3,2,0:T(8,128)(2,1)S(1)} %bitcast.117, f32[4,3,512,512]{2,3,1,0:T(8,128)} %get-tuple-element.25, f32[4,3,512]{2,1,0:T(4,128)S(1)} %get-tuple-element.24), kind=kOutput, calls=%fused_computation.51 | convolution fusion | flops 409337856 | bytes 14180352 | tf_op jit(solution)/shard_map/phqk,pkhd->pqhd/dot_general | solution.py:34
  393.5 1.6 copy.74
  395.1 18.5 %all_to_all.42 = bf16[4,512,192]{2,0,1:T(4,128)(2,1)} all-to-all(bf16[4,512,192]{2,0,1:T(4,128)(2,1)S(1)} %copy.74), channel_id=1, replica_groups=mesh['pairs'=32,'side'=2,'mp'=4] {'mp'}, dimensions={1} | all-to-all | bytes 1572864 | tf_op jit(solution)/shard_map/all_to_all | solution.py:52
  413.6 1.7 copy.76
  415.3 2.2 fusion.79
  417.5 0.3 multiply_reduce_fusion.2
  417.9 1.1 copy-done.3
  418.9 2.1 fusion.48
  (35 shorter events, 0.3 us)
Async XLA Ops:
  6.5 2.8 copy-start
  21.4 12.1 %copy-start.2 = (f32[1,4,768]{2,1,0:T(4,128)S(1)}, f32[1,4,768]{2,1,0:T(4,128)}, u32[]{:S(2)}) copy-start(f32[1,4,768]{2,1,0:T(4,128)} %param.18) | copy-start | bytes 36868
  21.4 197.7 %all-to-all-start = ((bf16[32,1,128,1024]{3,2,1,0:T(8,128)(2,1)}), bf16[32,1,128,1024]{3,2,1,0:T(8,128)(2,1)}, u32[]{:S(2)}, u32[]{:S(2)}) async-start(bf16[32,1,128,1024]{3,2,1,0:T(8,128)(2,1)} %bitcast_select_fusion), calls=%async_computation | async-start | bytes 16777216 | tf_op jit(solution)/shard_map/all_to_all | solution.py:96
  33.2 240.0 %all-gather.4.cloned.1.call-start = ((), (), s32[]{:S(2)}) async-start(), calls=%async_computation.3 | async-start | bytes 3932160 | tf_op jit(solution)/shard_map/all_gather | solution.py:43
  227.2 103.6 %all-gather.6.cloned.1.call-start = ((), (), s32[]{:S(2)}) async-start(), calls=%async_computation.4 | async-start | bytes 3932160 | tf_op jit(solution)/shard_map/all_gather | solution.py:43
  227.2 2.4 collective-permute-start
  229.8 43.4 %copy-start.4 = (bf16[1,3,768,192]{2,3,1,0:T(8,128)(2,1)S(1)}, bf16[1,3,768,192]{2,3,1,0:T(8,128)(2,1)}, u32[]{:S(2)}) copy-start(bf16[1,3,768,192]{2,3,1,0:T(8,128)(2,1)} %param.13) | copy-start | bytes 2654212
  231.4 141.4 %all-gather.8.cloned.1.call-start = ((), (), s32[]{:S(2)}) async-start(), calls=%async_computation.5 | async-start | bytes 3932160 | tf_op jit(solution)/shard_map/all_gather | solution.py:43
  329.5 1.2 copy-start.5
  334.0 38.7 %copy-start.6 = (bf16[1,768,192]{1,2,0:T(8,128)(2,1)S(1)}, bf16[1,768,192]{1,2,0:T(8,128)(2,1)}, u32[]{:S(2)}) copy-start(bf16[1,768,192]{1,2,0:T(8,128)(2,1)} %param.15) | copy-start | bytes 884740
  417.5 1.4 copy-start.3
  417.9 3.2 copy-start.1
Sparse Core Ops, SparseCore 0:
  227.3 45.8 all-gather.3
  275.0 53.5 all-gather.5
  330.8 41.9 all-gather.7
where the time goes:
time: 428 us
  waiting for transfers between devices  267 us (62%)
  matrix products  53.2 us (12%)
  blocking collectives  48.8 us (11%)
  local copies, waits for them, and re-layouts  18.4 us (4%)
  other arithmetic  14.4 us (3%)
  between operations  13.4 us (3%)
  starting transfers between devices  12 us (3%)
    all_to_all x1, waiting for transfers between devices, local(): lax.all_to_all(packet, 'pairs', split_axis=0, concat_axis=0, tiled=True)  186 us
    all_gather x3, waiting for transfers between devices, collect(): lax.all_gather(row_block, 'mp', axis=1, tiled=True)  79.5 us
    all_to_all x2, blocking collectives, to_rows(): lax.all_to_all(attended, 'mp', split_axis=1, concat_axis=2, tiled=True)  48.8 us
    sub x2, matrix products, attend_heads(): weights = jax.nn.softmax(scores, axis=-1).astype(jnp.bfloat16)  20.1 us
    dot_general x2, matrix products, attend_heads(): jnp.einsum('phqk,pkhd->pqhd', weights, value_rows.reshape(shaped), prefer...  12.7 us
    all_to_all x1, starting transfers between devices, local(): lax.all_to_all(packet, 'pairs', split_axis=0, concat_axis=0, tiled=True)  11.8 us
    dot_general x3, matrix products, collect(): jnp.einsum('prd,cde->prce', lax.all_gather(row_block, 'mp', axis=1, tiled...  11.2 us
  transfers between devices with their start and end apart: 5, of which 4 were waited for; matrix products, arithmetic and copies ran while one was open for 8% of the time, Pallas kernels for 0%

commit v1 on v0

v1 whole, which is shorter than its diff:
```python
import jax
import jax.numpy as jnp
from jax import lax
from jax.experimental import pallas as pl
from jax.experimental.pallas import tpu as pltpu
from jax.sharding import PartitionSpec as P

D = 768
HEADS = 12
HEAD_DIM = D // HEADS
TOK = 512
MP = 4
COLS = D // MP
WINDOW = 256
KINDS = 3
PIECE_ROWS = 8
PIECE_COLS = 384
HALVES = D // PIECE_COLS
LOG_SCALE = 1.4426950408889634 * HEAD_DIM**-0.5
VMEM = 48 * 2**20
MOST_VMEM = 61 * 2**20


def layer_norm(values, gain):
    average = jnp.mean(values, axis=-1, keepdims=True)
    centred = values - average
    spread = jnp.mean(centred * centred, axis=-1, keepdims=True)
    return centred * lax.rsqrt(spread + 1e-06) * gain


def estimate(flops, moved, exps=0):
    return pl.CostEstimate(flops=int(flops), bytes_accessed=int(moved), transcendentals=int(exps))


def embed_kernel(side_ref, tokens_ref, weight_ref, out_ref, held_ref, held_weight_ref, sems):
    views, rows, width = held_ref.shape
    fetched = pltpu.make_async_copy(tokens_ref.at[pl.ds(side_ref[0] * views, views)], held_ref, sems.at[0])
    fetched.start()
    halves = []
    for half in range(HALVES):
        columns = slice(half * PIECE_COLS, (half + 1) * PIECE_COLS)
        halves.append(
            pltpu.make_async_copy(weight_ref.at[:, columns], held_weight_ref.at[:, columns], sems.at[1 + half])
        )
        halves[half].start()
    fetched.wait()
    tokens = held_ref[...].reshape(views * rows, width)
    for half in range(HALVES):
        halves[half].wait()
        columns = slice(half * PIECE_COLS, (half + 1) * PIECE_COLS)
        embedded = jnp.dot(tokens, held_weight_ref[:, columns], preferred_element_type=jnp.float32)
        for view in range(views):
            for block in range(rows // PIECE_ROWS):
                top = view * rows + block * PIECE_ROWS
                out_ref[block * HALVES + half, view] = embedded[top : top + PIECE_ROWS].astype(jnp.bfloat16)


def embed(enc_tokens, embed_weight, side_index):
    views, rows, width = enc_tokens.shape
    taken = views // 2
    pieces = rows // PIECE_ROWS * HALVES
    return pl.pallas_call(
        embed_kernel,
        out_shape=jax.ShapeDtypeStruct((pieces, taken, PIECE_ROWS, PIECE_COLS), jnp.bfloat16),
        in_specs=[pl.BlockSpec(memory_space=pltpu.SMEM)] + [pl.BlockSpec(memory_space=pltpu.HBM)] * 2,
        out_specs=pl.BlockSpec(memory_space=pltpu.VMEM),
        scratch_shapes=[
            pltpu.VMEM((taken, rows, width), jnp.bfloat16),
            pltpu.VMEM((width, D), jnp.bfloat16),
            pltpu.SemaphoreType.DMA((1 + HALVES,)),
        ],
        compiler_params=pltpu.CompilerParams(vmem_limit_bytes=MOST_VMEM),
        cost_estimate=estimate(2 * taken * rows * width * D, 2 * (taken * rows * (width + D) + width * D)),
        name="embed",
    )(side_index.reshape(1), enc_tokens, embed_weight)


def pick_kernel(slots_ref, own_ref, other_ref, out_ref):
    count = own_ref.shape[0]

    def step(pair, carry):
        code = slots_ref[pair]
        foreign = code >= count
        slot = jnp.where(foreign, code - count, code)
        out_ref[pair] = jnp.where(foreign, other_ref[slot], own_ref[slot])
        return carry

    lax.fori_loop(0, out_ref.shape[0], step, 0, unroll=8)


def pick(slots, own, other):
    shape = (slots.shape[0],) + own.shape[1:]
    return pl.pallas_call(
        pick_kernel,
        out_shape=jax.ShapeDtypeStruct(shape, own.dtype),
        in_specs=[
            pl.BlockSpec(memory_space=pltpu.SMEM),
            pl.BlockSpec(memory_space=pltpu.VMEM),
            pl.BlockSpec(memory_space=pltpu.VMEM),
        ],
        out_specs=pl.BlockSpec(memory_space=pltpu.VMEM),
        compiler_params=pltpu.CompilerParams(vmem_limit_bytes=VMEM),
        cost_estimate=estimate(own.size, 6 * own.size),
        name="pick",
    )(slots, own, other)


def unpack(pieces_ref, rows_ref):
    per_device = TOK // MP
    for piece in range(pieces_ref.shape[0]):
        source, owner = divmod(piece, MP)
        block, half = divmod(source, HALVES)
        top = owner * per_device + block * PIECE_ROWS
        rows_ref[top : top + PIECE_ROWS, half * PIECE_COLS : (half + 1) * PIECE_COLS] = pieces_ref[
            piece
        ].astype(jnp.float32)


def normalise(rows_ref, gain, out_ref):
    for top in range(0, TOK, 128):
        out_ref[top : top + 128] = layer_norm(rows_ref[top : top + 128], gain).astype(jnp.bfloat16)


def project(rows, weight_ref, kind, quad):
    parts = []
    column = quad * WINDOW
    while column < (quad + 1) * WINDOW:
        owner, first = divmod(column, COLS)
        last = min(COLS, first + (quad + 1) * WINDOW - column)
        parts.append(weight_ref[owner, kind, first:last])
        column += last - first
    return lax.dot_general(
        rows, jnp.concatenate(parts, axis=0), (((1,), (1,)), ((), ())), preferred_element_type=jnp.float32
    )


def attend(queries, keys, values):
    lane = lax.broadcasted_iota(jnp.int32, (1, WINDOW), 1)
    keys = keys.astype(jnp.bfloat16)
    values = values.astype(jnp.bfloat16)
    attended = jnp.zeros(queries.shape, jnp.float32)
    for head in range(WINDOW // HEAD_DIM):
        inside = lane // HEAD_DIM == head
        masked = jnp.where(inside, queries, 0.0).astype(jnp.bfloat16)
        scores = lax.dot_general(
            masked, keys, (((1,), (1,)), ((), ())), preferred_element_type=jnp.float32
        )
        scores = scores * LOG_SCALE
        weights = jnp.exp2(scores - jnp.max(scores, axis=-1, keepdims=True))
        total = jnp.sum(weights, axis=-1, keepdims=True)
        mixture = jnp.dot(weights.astype(jnp.bfloat16), values, preferred_element_type=jnp.float32)
        attended = jnp.where(inside, mixture * (1.0 / total), attended)
    return attended.astype(jnp.bfloat16)


def self_kernel(
    pieces_ref, gathered_ref, out_weight_ref, gain_ref, out_ref, normed_ref, attended_ref, weight_ref, sem
):
    fetched = pltpu.make_async_copy(gathered_ref.at[:, 0:KINDS], weight_ref, sem)
    fetched.start()
    unpack(pieces_ref, out_ref)
    normalise(out_ref, gain_ref[0:1], normed_ref)
    normed = normed_ref[...]
    fetched.wait()
    for quad in range(D // WINDOW):
        attended_ref[:, quad * WINDOW : (quad + 1) * WINDOW] = attend(
            *(project(normed, weight_ref, kind, quad) for kind in range(KINDS))
        )
    out_ref[...] += jnp.dot(attended_ref[...], out_weight_ref[...], preferred_element_type=jnp.float32)


def cross_kernel(
    after_ref,
    pieces_ref,
    gathered_ref,
    out_weight_ref,
    gain_ref,
    out_ref,
    rows_ref,
    query_ref,
    partner_ref,
    attended_ref,
    weight_ref,
    sem,
):
    fetched = pltpu.make_async_copy(gathered_ref.at[:, KINDS : 2 * KINDS], weight_ref, sem)
    fetched.start()
    unpack(pieces_ref, rows_ref)
    normalise(rows_ref, gain_ref[2:3], partner_ref)
    normalise(after_ref, gain_ref[1:2], query_ref)
    queries, partner = query_ref[...], partner_ref[...]
    fetched.wait()
    for quad in range(D // WINDOW):
        attended_ref[:, quad * WINDOW : (quad + 1) * WINDOW] = attend(
            project(queries, weight_ref, 0, quad),
            project(partner, weight_ref, 1, quad),
            project(partner, weight_ref, 2, quad),
        )
    rows_ref[...] = after_ref[...] + jnp.dot(
        attended_ref[...], out_weight_ref[...], preferred_element_type=jnp.float32
    )
    normalise(rows_ref, gain_ref[3:4], out_ref)


def in_vmem(count):
    return [pl.BlockSpec(memory_space=pltpu.VMEM)] * count


def in_hbm(count):
    return [pl.BlockSpec(memory_space=pltpu.HBM)] * count


def fetched_weights():
    return [pltpu.VMEM((MP, KINDS, COLS, D), jnp.bfloat16), pltpu.SemaphoreType.DMA]


def self_block(pieces, weights, out_weight, gains):
    return pl.pallas_call(
        self_kernel,
        out_shape=jax.ShapeDtypeStruct((TOK, D), jnp.float32),
        in_specs=in_vmem(1) + [pl.BlockSpec(memory_space=pltpu.HBM)] + in_vmem(2),
        out_specs=in_vmem(1)[0],
        scratch_shapes=[pltpu.VMEM((TOK, D), jnp.bfloat16)] * 2 + fetched_weights(),
        compiler_params=pltpu.CompilerParams(vmem_limit_bytes=VMEM),
        cost_estimate=estimate(8 * TOK * D * D + 4 * TOK * TOK * D, 8 * 2**20, HEADS * TOK * TOK),
        name="self_block",
    )(pieces, weights, out_weight, gains)


def cross_block(after_self, pieces, weights, out_weight, gains):
    return pl.pallas_call(
        cross_kernel,
        out_shape=jax.ShapeDtypeStruct((TOK, D), jnp.bfloat16),
        in_specs=in_vmem(2) + [pl.BlockSpec(memory_space=pltpu.HBM)] + in_vmem(2),
        out_specs=in_vmem(1)[0],
        scratch_shapes=[pltpu.VMEM((TOK, D), jnp.float32)] + [pltpu.VMEM((TOK, D), jnp.bfloat16)] * 3 + fetched_weights(),
        compiler_params=pltpu.CompilerParams(vmem_limit_bytes=VMEM),
        cost_estimate=estimate(8 * TOK * D * D + 4 * TOK * TOK * D, 8 * 2**20, HEADS * TOK * TOK),
        name="cross_block",
    )(after_self, pieces, weights, out_weight, gains)


def together_kernel(*refs):
    *sources, out_ref, held_ref, in_sems, out_sems = refs
    arriving = []
    for source in sources:
        for kind in range(source.shape[0]):
            place = len(arriving)
            arriving.append(pltpu.make_async_copy(source.at[kind], held_ref.at[place], in_sems.at[place]))
            arriving[place].start()
    leaving = []
    for place, copy in enumerate(arriving):
        copy.wait()
        leaving.append(pltpu.make_async_copy(held_ref.at[place], out_ref.at[place], out_sems.at[place]))
        leaving[place].start()
    for copy in leaving:
        copy.wait()


def together(*weights):
    count = sum(weight.shape[0] for weight in weights)
    shape = (count,) + weights[0].shape[1:]
    return pl.pallas_call(
        together_kernel,
        out_shape=jax.ShapeDtypeStruct(shape, jnp.bfloat16),
        in_specs=in_hbm(len(weights)),
        out_specs=in_hbm(1)[0],
        scratch_shapes=[
            pltpu.VMEM(shape, jnp.bfloat16),
            pltpu.SemaphoreType.DMA((count,)),
            pltpu.SemaphoreType.DMA((count,)),
        ],
        compiler_params=pltpu.CompilerParams(vmem_limit_bytes=MOST_VMEM),
        cost_estimate=estimate(0, 4 * count * COLS * D),
        name="together",
    )(*weights)


def local(
    enc_tokens,
    pair_views,
    embed_weight,
    self_qkv,
    self_out,
    cross_query,
    cross_kv,
    cross_out,
    norm_gains,
    head_weight,
):
    side_index = lax.axis_index("side")
    flip = [(0, 1), (1, 0)]
    weights = together(*(jnp.swapaxes(weight, 1, 2) for weight in (self_qkv[0], cross_query, cross_kv[0])))
    weights = lax.all_gather(weights, "mp", axis=0)
    spread = lax.all_to_all(
        embed(enc_tokens, embed_weight, side_index), "pairs", split_axis=0, concat_axis=0, tiled=True
    )
    views = enc_tokens.shape[0]
    taken = views // 2
    own = spread.reshape((-1,) + spread.shape[2:])
    other = lax.ppermute(own, "side", flip)
    wanted = jnp.where(side_index == 0, pair_views[:, 0], pair_views[:, 1])
    within = wanted % views
    slots = wanted // views * taken + within % taken
    slots = jnp.where(within // taken == side_index, slots, slots + own.shape[0])
    packets = pick(slots, own, other)
    pieces = lax.all_to_all(packets, ("pairs", "mp"), split_axis=0, concat_axis=0, tiled=True)
    partner = lax.ppermute(pieces, "side", flip)
    after_self = self_block(pieces, weights, self_out[0], norm_gains[0])
    final_rows = cross_block(after_self, partner, weights, cross_out[0], norm_gains[0])
    final_rows = lax.all_to_all(
        final_rows.reshape(MP, TOK // MP, D), "mp", split_axis=0, concat_axis=0, tiled=True
    )
    result = jnp.einsum("prd,de->pre", final_rows, head_weight[0], preferred_element_type=jnp.float32)
    return result.astype(jnp.bfloat16)[:, None]


def solution(mesh):
    placed = (
        P("pairs", "mp", None),
        P(),
        P(),
        P("side", None, None, "mp"),
        P("side", None, None),
        P("side", None, "mp"),
        P("side", None, None, "mp"),
        P("side", None, None),
        P("side", None, None),
        P("side", None, None),
    )
    return jax.shard_map(
        local, mesh=mesh, in_specs=placed, out_specs=P("pairs", "side", "mp", None), check_vma=False
    )
```

time: 428 us -> 142 us (0.33)
  waiting for transfers between devices: 267 us -> 11.8 us
  matrix products: 53.2 us -> 1.95 us
  blocking collectives: 48.8 us -> 85 us
  Pallas kernels: 0 us -> 28.4 us
  local copies, waits for them, and re-layouts: 18.4 us -> 1.29 us
  other arithmetic: 14.4 us -> 0.02 us
  starting transfers between devices: 12 us -> 0.01 us
    all_to_all x1 -> x0, waiting for transfers between devices: 186 us -> none  [local(): lax.all_to_all(packet, 'pairs', split_axis=0, concat_axis=0, tiled=True)]
    all_gather x3 -> x1, waiting for transfers between devices: 79.5 us -> 9.41 us  [local(): weights = lax.all_gather(weights, 'mp', axis=0)]
    all_to_all x2 -> x3, blocking collectives: 48.8 us -> 85 us  [the longest x1 35 us: local(): lax.all_to_all(packets, ('pairs', 'mp'), split_axis=0, concat_axis=0, til...]
    dot_general x8 -> x0, matrix products: 31 us -> none  [the longest x2 12.7 us: attend_heads(): jnp.einsum('phqk,pkhd->pqhd', weights, value_rows.reshape(shaped), prefer...]
    pallas_call x0 -> x5, Pallas kernels: none -> 28.4 us  [the longest x1 11.1 us: cross_block(): pl.pallas_call(cross_kernel, out_shape=jax.ShapeDtypeStruct((TOK, D), jnp...]
    sub x2 -> x0, matrix products: 20.1 us -> none  [attend_heads(): weights = jax.nn.softmax(scores, axis=-1).astype(jnp.bfloat16)]
    all_to_all x1 -> x0, starting transfers between devices: 11.8 us -> none  [local(): lax.all_to_all(packet, 'pairs', split_axis=0, concat_axis=0, tiled=True)]
    gather x2 -> x0, local copies, waits for them, and re-layouts: 8.81 us -> none  [the longest x1 4.82 us: local(): enc_tokens[source]]
  transfers between devices with their start and end apart: 5 -> 3, of which waited for: 4 -> 2; matrix products, arithmetic and copies ran while one was open for 8% -> 0% of each run, Pallas kernels for 0% -> 10%
where the time goes in v1:
time: 142 us
  blocking collectives  85 us (60%)
  Pallas kernels  28.4 us (20%)
  between operations  13.5 us (10%)
  waiting for transfers between devices  11.8 us (8%)
  matrix products  1.95 us (1%)
    all_to_all x1, blocking collectives, local(): lax.all_to_all(packets, ('pairs', 'mp'), split_axis=0, concat_axis=0, til...  35 us
    all_to_all x1, blocking collectives, local(): lax.all_to_all(embed(enc_tokens, embed_weight, side_index), 'pairs', spli...  34.1 us
    all_to_all x1, blocking collectives, local(): lax.all_to_all(final_rows.reshape(MP, TOK // MP, D), 'mp', split_axis=0,...  15.9 us
    pallas_call x1, Pallas kernels, cross_block(): pl.pallas_call(cross_kernel, out_shape=jax.ShapeDtypeStruct((TOK, D), jnp...  11.1 us
    pallas_call x1, Pallas kernels, self_block(): pl.pallas_call(self_kernel, out_shape=jax.ShapeDtypeStruct((TOK, D), jnp....  9.52 us
    all_gather x1, waiting for transfers between devices, local(): weights = lax.all_gather(weights, 'mp', axis=0)  9.41 us
    pallas_call x1, Pallas kernels, embed(): pl.pallas_call(embed_kernel, out_shape=jax.ShapeDtypeStruct((pieces, take...  3.77 us
  transfers between devices with their start and end apart: 3, of which 2 were waited for; matrix products, arithmetic and copies ran while one was open for 0% of the time, Pallas kernels for 10%

profile of v1, /device:TPU:2, one launch (start us, length us, event | category | flops | bytes accessed | tf_op | source)
XLA Modules:
  0.0 141.9 jit_solution(8297198563260403378)
XLA Ops:
  6.5 0.0 copy-start
  6.5 0.0 all-gather.3.cloned.1.call-start
  6.5 2.5 %together.1 = bf16[6,192,768]{2,1,0:T(8,128)(2,1)} custom-call(bf16[3,192,768]{2,1,0:T(8,128)(2,1)} %bitcast.38, bf16[1,192,768]{2,1,0:T(8,128)(2,1)} %bitcast.40, bf16[2,192,768]{2,1,0:T(8,128)(2,1)} %bitcast.39), custom_call_target="tpu_custom_call" | custom-call | bytes 3538944 | tf_op jit(solution)/shard_map/together/pallas_call | solution.py:263
  9.0 0.0 all-gather.3.cloned.1.call-update
  9.1 3.8 %embed.1 = bf16[32,4,8,384]{3,2,1,0:T(8,128)(2,1)} custom-call(s32[1]{0:T(128)} %bitcast.1.side_ref, bf16[8,128,1024]{2,1,0:T(8,128)(2,1)} %tokens_ref.1, bf16[1024,768]{1,0:T(8,128)(2,1)} %weight_ref.1), custom_call_target="tpu_custom_call" | custom-call | flops 805306368 | bytes 3407872 | tf_op jit(solution)/shard_map/embed/pallas_call | solution.py:62
  12.8 0.0 copy-start.4
  12.9 34.1 %all_to_all.15 = bf16[32,4,8,384]{3,2,1,0:T(8,128)(2,1)S(1)} all-to-all(bf16[32,4,8,384]{3,2,1,0:T(8,128)(2,1)} %embed.1), channel_id=1, replica_groups=mesh['pairs'=32,'side'=2,'mp'=4] {'pairs'}, dimensions={0} | all-to-all | bytes 1572864 | tf_op jit(solution)/shard_map/all_to_all | solution.py:295
  46.9 0.0 collective-permute-start
  46.9 0.0 copy-done.4
  47.0 0.0 copy-start.3
  47.0 2.4 %collective-permute-done.other_ref = bf16[128,8,384]{2,1,0:T(8,128)(2,1)} collective-permute-done((bf16[128,8,384]{2,1,0:T(8,128)(2,1)S(1)}, bf16[128,8,384]{2,1,0:T(8,128)(2,1)}, u32[]{:S(2)}, u32[]{:S(2)}) %collective-permute-start) | collective-permute-done | bytes 786464 | tf_op jit(solution)/shard_map/ppermute | solution.py:301
  49.3 1.6 %pick.1 = bf16[128,8,384]{2,1,0:T(8,128)(2,1)S(1)} custom-call(s32[128]{0:T(128)S(1)} %compare_select_fusion.slots_ref, bf16[128,8,384]{2,1,0:T(8,128)(2,1)S(1)} %bitcast.32, bf16[128,8,384]{2,1,0:T(8,128)(2,1)} %collective-permute-done.other_ref), custom_call_target="tpu_custom_call" | custom-call | flops 393216 | bytes 2359296 | tf_op jit(solution)/shard_map/pick/pallas_call | solution.py:93
  50.9 35.0 %all_to_all.16.pieces_ref = bf16[128,8,384]{2,1,0:T(8,128)(2,1)S(1)} all-to-all(bf16[128,8,384]{2,1,0:T(8,128)(2,1)S(1)} %pick.1), channel_id=1, replica_groups=mesh['pairs'=32,'side'=2,'mp'=4] {'pairs','mp'}, dimensions={0} | all-to-all | bytes 1572864 | tf_op jit(solution)/shard_map/all_to_all | solution.py:307
  85.9 0.0 collective-permute-start.1
  86.0 9.4 %all-gather.3.cloned.1.call-done = bf16[24,192,768]{2,1,0:T(8,128)(2,1)} async-done(((bf16[6,192,768]{2,1,0:T(8,128)(2,1)}), bf16[24,192,768]{2,1,0:T(8,128)(2,1)}) %all-gather.3.cloned.1.call-update) | async-done | bytes 7077904 | tf_op jit(solution)/shard_map/all_gather | solution.py:294
  95.4 0.0 copy-done.3
  95.4 0.0 copy-start.1
  95.4 1.3 copy-done.1
  96.6 0.0 copy-start.2
  96.6 9.5 %self_block.1.after_ref = f32[512,768]{1,0:T(8,128)S(1)} custom-call(bf16[128,8,384]{2,1,0:T(8,128)(2,1)S(1)} %all_to_all.16.pieces_ref, bf16[4,6,192,768]{3,2,1,0:T(8,128)(2,1)} %bitcast.41, bf16[768,768]{1,0:T(8,128)(2,1)S(1)} %bitcast.34, f32[4,768]{1,0:T(4,128)S(1)} %bitcast.36), custom_call_target="tpu_custom_call" | custom-call | flops 3221225472 | bytes 8388608 | tf_op jit(solution)/shard_map/self_block/pallas_call | solution.py:218
  106.2 0.0 collective-permute-done.1.pieces_ref
  106.2 0.0 copy-done.2
  106.2 11.1 %cross_block.1 = bf16[512,768]{1,0:T(8,128)(2,1)S(1)} custom-call(f32[512,768]{1,0:T(8,128)S(1)} %self_block.1.after_ref, bf16[128,8,384]{2,1,0:T(8,128)(2,1)} %collective-permute-done.1.pieces_ref, bf16[4,6,192,768]{3,2,1,0:T(8,128)(2,1)} %bitcast.42, bf16[768,768]{1,0:T(8,128)(2,1)S(1)} %bitcast.35, f32[4,768]{1,0:T(4,128)S(1)} %bitcast.37), custom_call_target="tpu_custom_call" | custom-call | flops 3221225472 | bytes 8388608 | tf_op jit(solution)/shard_map/cross_block/pallas_call | solution.py:231
  117.3 15.9 %all_to_all.17 = bf16[4,128,768]{2,1,0:T(8,128)(2,1)S(1)} all-to-all(bf16[4,128,768]{2,1,0:T(8,128)(2,1)S(1)} %bitcast.33), channel_id=1, replica_groups=mesh['pairs'=32,'side'=2,'mp'=4] {'mp'}, dimensions={0} | all-to-all | bytes 1572864 | tf_op jit(solution)/shard_map/all_to_all | solution.py:311
  133.1 0.0 copy-done
  133.1 2.0 %fusion.5 = bf16[4,1,128,1024]{3,2,1,0:T(8,128)(2,1)} fusion(bf16[4,128,768]{2,1,0:T(8,128)(2,1)S(1)} %all_to_all.17, bf16[1,768,1024]{2,1,0:T(8,128)(2,1)S(1)} %copy-done), kind=kOutput, calls=%fused_computation.3 | convolution fusion | flops 805830656 | bytes 3407872 | tf_op jit(solution)/shard_map/prd,de->pre/dot_general | solution.py:314
  (1 shorter events, 0.0 us)
Async XLA Ops:
  6.5 126.6 %copy-start = (bf16[1,768,1024]{2,1,0:T(8,128)(2,1)S(1)}, bf16[1,768,1024]{2,1,0:T(8,128)(2,1)}, u32[]{:S(2)}) copy-start(bf16[1,768,1024]{2,1,0:T(8,128)(2,1)} %param.19) | copy-start | bytes 4718596
  6.5 88.8 %all-gather.3.cloned.1.call-start = ((), (), s32[]{:S(2)}) async-start(), calls=%async_computation.3 | async-start | bytes 8847360 | tf_op jit(solution)/shard_map/all_gather | solution.py:294
  12.8 34.1 %copy-start.4 = (s32[128,2]{0,1:T(2,128)S(1)}, s32[128,2]{0,1:T(2,128)}, u32[]{:S(2)}) copy-start(s32[128,2]{0,1:T(2,128)} %param.11) | copy-start | bytes 3076
  46.9 2.4 %collective-permute-start = (bf16[128,8,384]{2,1,0:T(8,128)(2,1)S(1)}, bf16[128,8,384]{2,1,0:T(8,128)(2,1)}, u32[]{:S(2)}, u32[]{:S(2)}) collective-permute-start(bf16[128,8,384]{2,1,0:T(8,128)(2,1)S(1)} %bitcast.31), channel_id=1, source_target_pairs={{0,4},{4,0},{1,5},{5,1},{2,6},{6,2},{3,7},{7,3},{8,12},{12,8},{9,1... | collective-permute-start | bytes 2359304 | tf_op jit(solution)/shard_map/ppermute | solution.py:301
  47.0 48.4 %copy-start.3 = (f32[1,4,768]{2,1,0:T(4,128)S(1)}, f32[1,4,768]{2,1,0:T(4,128)}, u32[]{:S(2)}) copy-start(f32[1,4,768]{2,1,0:T(4,128)} %param.18) | copy-start | bytes 36868
  85.9 20.2 %collective-permute-start.1 = (bf16[128,8,384]{2,1,0:T(8,128)(2,1)S(1)}, bf16[128,8,384]{2,1,0:T(8,128)(2,1)}, u32[]{:S(2)}, u32[]{:S(2)}) collective-permute-start(bf16[128,8,384]{2,1,0:T(8,128)(2,1)S(1)} %all_to_all.16.pieces_ref), channel_id=1, source_target_pairs={{0,4},{4,0},{1,5},{5,1},{2,6},{6,2},{3,7},{7,3},{8,12},{12,8},{9,1... | collective-permute-start | bytes 2359304 | tf_op jit(solution)/shard_map/ppermute | solution.py:308
  95.4 1.3 copy-start.1
  96.6 9.5 %copy-start.2 = (bf16[1,768,768]{2,1,0:T(8,128)(2,1)S(1)}, bf16[1,768,768]{2,1,0:T(8,128)(2,1)}, u32[]{:S(2)}) copy-start(bf16[1,768,768]{2,1,0:T(8,128)(2,1)} %param.17) | copy-start | bytes 3538948
Sparse Core Ops, SparseCore 0:
  9.2 86.1 all-gather.2

commit v2 on v1

--- a/solution.py
+++ b/solution.py
@@ -16,6 +16,9 @@
 PIECE_ROWS = 8
 PIECE_COLS = 384
 HALVES = D // PIECE_COLS
+APART = (0, -1 % MP, 1, 2)
+CHUNK = 512
+AHEAD = 1
 LOG_SCALE = 1.4426950408889634 * HEAD_DIM**-0.5
 VMEM = 48 * 2**20
 MOST_VMEM = 61 * 2**20
@@ -30,6 +33,14 @@
 
 def estimate(flops, moved, exps=0):
     return pl.CostEstimate(flops=int(flops), bytes_accessed=int(moved), transcendentals=int(exps))
+
+
+def in_vmem(count):
+    return [pl.BlockSpec(memory_space=pltpu.VMEM)] * count
+
+
+def in_hbm(count):
+    return [pl.BlockSpec(memory_space=pltpu.HBM)] * count
 
 
 def embed_kernel(side_ref, tokens_ref, weight_ref, out_ref, held_ref, held_weight_ref, sems):
@@ -121,123 +132,167 @@
         out_ref[top : top + 128] = layer_norm(rows_ref[top : top + 128], gain).astype(jnp.bfloat16)
 
 
-def project(rows, weight_ref, kind, quad):
+def project(rows, columns_of, quad):
     parts = []
     column = quad * WINDOW
     while column < (quad + 1) * WINDOW:
         owner, first = divmod(column, COLS)
         last = min(COLS, first + (quad + 1) * WINDOW - column)
-        parts.append(weight_ref[owner, kind, first:last])
+        parts.append(columns_of(owner, first, last))
         column += last - first
     return lax.dot_general(
         rows, jnp.concatenate(parts, axis=0), (((1,), (1,)), ((), ())), preferred_element_type=jnp.float32
     )
 
 
-def attend(queries, keys, values):
+def of_kind(weight_ref, kind):
+    return lambda owner, first, last: weight_ref[owner, kind, first:last]
+
+
+def scores_of(queries, keys, head, top):
+    inside = lax.broadcasted_iota(jnp.int32, (1, WINDOW), 1) // HEAD_DIM == head
+    masked = jnp.where(inside, queries[top : top + CHUNK], 0.0).astype(jnp.bfloat16)
+    return lax.dot_general(masked, keys, (((1,), (1,)), ((), ())), preferred_element_type=jnp.float32)
+
+
+def attend(quad_of, attended_ref):
+    steps = [
+        (quad, head, top)
+        for quad in range(D // WINDOW)
+        for head in range(WINDOW // HEAD_DIM)
+        for top in range(0, TOK, CHUNK)
+    ]
     lane = lax.broadcasted_iota(jnp.int32, (1, WINDOW), 1)
-    keys = keys.astype(jnp.bfloat16)
-    values = values.astype(jnp.bfloat16)
-    attended = jnp.zeros(queries.shape, jnp.float32)
-    for head in range(WINDOW // HEAD_DIM):
-        inside = lane // HEAD_DIM == head
-        masked = jnp.where(inside, queries, 0.0).astype(jnp.bfloat16)
-        scores = lax.dot_general(
-            masked, keys, (((1,), (1,)), ((), ())), preferred_element_type=jnp.float32
-        )
-        scores = scores * LOG_SCALE
+    held = {}
+    sums = {}
+
+    def start(step):
+        quad, head, top = step
+        if quad not in held:
+            queries, keys, values = quad_of(quad)
+            held[quad] = (queries * LOG_SCALE, keys.astype(jnp.bfloat16), values.astype(jnp.bfloat16))
+        return scores_of(held[quad][0], held[quad][1], head, top)
+
+    ahead = [start(step) for step in steps[:AHEAD]]
+    for count, (quad, head, top) in enumerate(steps):
+        if count + AHEAD < len(steps):
+            ahead.append(start(steps[count + AHEAD]))
+        scores = ahead.pop(0)
         weights = jnp.exp2(scores - jnp.max(scores, axis=-1, keepdims=True))
         total = jnp.sum(weights, axis=-1, keepdims=True)
-        mixture = jnp.dot(weights.astype(jnp.bfloat16), values, preferred_element_type=jnp.float32)
-        attended = jnp.where(inside, mixture * (1.0 / total), attended)
-    return attended.astype(jnp.bfloat16)
+        mixture = jnp.dot(weights.astype(jnp.bfloat16), held[quad][2], preferred_element_type=jnp.float32)
+        mixture = mixture * (1.0 / total)
+        if head:
+            mixture = jnp.where(lane // HEAD_DIM == head, mixture, sums[quad, top])
+        sums[quad, top] = mixture
+        if head == WINDOW // HEAD_DIM - 1:
+            attended_ref[top : top + CHUNK, quad * WINDOW : (quad + 1) * WINDOW] = mixture.astype(jnp.bfloat16)
 
 
 def self_kernel(
-    pieces_ref, gathered_ref, out_weight_ref, gain_ref, out_ref, normed_ref, attended_ref, weight_ref, sem
+    pieces_ref, gathered_ref, out_weight_ref, gain_ref, out_ref, cross_ref, normed_ref, attended_ref, weight_ref, sems
 ):
-    fetched = pltpu.make_async_copy(gathered_ref.at[:, 0:KINDS], weight_ref, sem)
-    fetched.start()
+    fetched = []
+    for owner in range(MP):
+        fetched.append(
+            pltpu.make_async_copy(gathered_ref.at[owner, 0:KINDS], weight_ref.at[owner], sems.at[owner])
+        )
+        fetched[owner].start()
+    passed = pltpu.make_async_copy(gathered_ref.at[:, KINDS:], cross_ref, sems.at[MP])
+    passed.start()
     unpack(pieces_ref, out_ref)
     normalise(out_ref, gain_ref[0:1], normed_ref)
     normed = normed_ref[...]
-    fetched.wait()
-    for quad in range(D // WINDOW):
-        attended_ref[:, quad * WINDOW : (quad + 1) * WINDOW] = attend(
-            *(project(normed, weight_ref, kind, quad) for kind in range(KINDS))
-        )
+    waited = []
+
+    def quad_of(quad):
+        while len(waited) <= (quad * WINDOW + WINDOW - 1) // COLS:
+            fetched[len(waited)].wait()
+            waited.append(True)
+        return [project(normed, of_kind(weight_ref, kind), quad) for kind in range(KINDS)]
+
+    attend(quad_of, attended_ref)
     out_ref[...] += jnp.dot(attended_ref[...], out_weight_ref[...], preferred_element_type=jnp.float32)
+    passed.wait()
 
 
 def cross_kernel(
-    after_ref,
-    pieces_ref,
-    gathered_ref,
-    out_weight_ref,
-    gain_ref,
-    out_ref,
-    rows_ref,
-    query_ref,
-    partner_ref,
-    attended_ref,
-    weight_ref,
-    sem,
+    place_ref, after_ref, pieces_ref, slices0_ref, slices1_ref, slices2_ref, slices3_ref, weight_ref, out_weight_ref,
+    gain_ref, out_ref, rows_ref, query_ref, partner_ref, attended_ref, slices_ref, sems,
 ):
-    fetched = pltpu.make_async_copy(gathered_ref.at[:, KINDS : 2 * KINDS], weight_ref, sem)
-    fetched.start()
+    fetched = []
+    for count, source in enumerate((slices0_ref, slices1_ref, slices2_ref, slices3_ref)):
+        along_x = lax.rem(place_ref[1] + APART[count], MP)
+        for place in range(MP):
+            owner = lax.rem(place_ref[0] + APART[place], MP)
+            sem = sems.at[count * MP + place]
+            fetched.append(pltpu.make_async_copy(source.at[place], slices_ref.at[owner, along_x], sem))
+            fetched[-1].start()
     unpack(pieces_ref, rows_ref)
     normalise(rows_ref, gain_ref[2:3], partner_ref)
     normalise(after_ref, gain_ref[1:2], query_ref)
     queries, partner = query_ref[...], partner_ref[...]
-    fetched.wait()
-    for quad in range(D // WINDOW):
-        attended_ref[:, quad * WINDOW : (quad + 1) * WINDOW] = attend(
-            project(queries, weight_ref, 0, quad),
-            project(partner, weight_ref, 1, quad),
-            project(partner, weight_ref, 2, quad),
-        )
+    for copy in fetched:
+        copy.wait()
+
+    def query_columns(owner, first, last):
+        return slices_ref[owner].reshape(COLS, D)[first:last]
+
+    attend(
+        lambda quad: (
+            project(queries, query_columns, quad),
+            project(partner, of_kind(weight_ref, 0), quad),
+            project(partner, of_kind(weight_ref, 1), quad),
+        ),
+        attended_ref,
+    )
     rows_ref[...] = after_ref[...] + jnp.dot(
         attended_ref[...], out_weight_ref[...], preferred_element_type=jnp.float32
     )
     normalise(rows_ref, gain_ref[3:4], out_ref)
 
 
-def in_vmem(count):
-    return [pl.BlockSpec(memory_space=pltpu.VMEM)] * count
-
-
-def in_hbm(count):
-    return [pl.BlockSpec(memory_space=pltpu.HBM)] * count
-
-
-def fetched_weights():
-    return [pltpu.VMEM((MP, KINDS, COLS, D), jnp.bfloat16), pltpu.SemaphoreType.DMA]
-
-
 def self_block(pieces, weights, out_weight, gains):
+    rest = weights.shape[1] - KINDS
     return pl.pallas_call(
         self_kernel,
-        out_shape=jax.ShapeDtypeStruct((TOK, D), jnp.float32),
-        in_specs=in_vmem(1) + [pl.BlockSpec(memory_space=pltpu.HBM)] + in_vmem(2),
-        out_specs=in_vmem(1)[0],
-        scratch_shapes=[pltpu.VMEM((TOK, D), jnp.bfloat16)] * 2 + fetched_weights(),
+        out_shape=(
+            jax.ShapeDtypeStruct((TOK, D), jnp.float32),
+            jax.ShapeDtypeStruct((MP, rest, COLS, D), jnp.bfloat16),
+        ),
+        in_specs=in_vmem(1) + in_hbm(1) + in_vmem(2),
+        out_specs=tuple(in_vmem(2)),
+        scratch_shapes=[pltpu.VMEM((TOK, D), jnp.bfloat16)] * 2
+        + [pltpu.VMEM((MP, KINDS, COLS, D), jnp.bfloat16), pltpu.SemaphoreType.DMA((MP + 1,))],
         compiler_params=pltpu.CompilerParams(vmem_limit_bytes=VMEM),
         cost_estimate=estimate(8 * TOK * D * D + 4 * TOK * TOK * D, 8 * 2**20, HEADS * TOK * TOK),
         name="self_block",
     )(pieces, weights, out_weight, gains)
 
 
-def cross_block(after_self, pieces, weights, out_weight, gains):
+def cross_block(place, after_self, pieces, slices, weights, out_weight, gains):
     return pl.pallas_call(
         cross_kernel,
         out_shape=jax.ShapeDtypeStruct((TOK, D), jnp.bfloat16),
-        in_specs=in_vmem(2) + [pl.BlockSpec(memory_space=pltpu.HBM)] + in_vmem(2),
+        in_specs=[pl.BlockSpec(memory_space=pltpu.SMEM)] + in_vmem(2) + in_hbm(MP) + in_vmem(3),
         out_specs=in_vmem(1)[0],
-        scratch_shapes=[pltpu.VMEM((TOK, D), jnp.float32)] + [pltpu.VMEM((TOK, D), jnp.bfloat16)] * 3 + fetched_weights(),
+        scratch_shapes=[pltpu.VMEM((TOK, D), jnp.float32)]
+        + [pltpu.VMEM((TOK, D), jnp.bfloat16)] * 3
+        + [pltpu.VMEM((MP,) + slices[0].shape, jnp.bfloat16), pltpu.SemaphoreType.DMA((MP * MP,))],
         compiler_params=pltpu.CompilerParams(vmem_limit_bytes=VMEM),
         cost_estimate=estimate(8 * TOK * D * D + 4 * TOK * TOK * D, 8 * 2**20, HEADS * TOK * TOK),
         name="cross_block",
-    )(after_self, pieces, weights, out_weight, gains)
+    )(place, after_self, pieces, *slices, weights, out_weight, gains)
+
+
+def from_mp(value, apart):
+    return lax.ppermute(value, "mp", [((index + apart) % MP, index) for index in range(MP)])
+
+
+def from_x(value, apart):
+    count = lax.axis_size("pairs")
+    pairs = [(index // MP * MP + (index + apart) % MP, index) for index in range(count)]
+    return lax.ppermute(value, "pairs", pairs)
 
 
 def together_kernel(*refs):
@@ -290,11 +345,16 @@
 ):
     side_index = lax.axis_index("side")
     flip = [(0, 1), (1, 0)]
-    weights = together(*(jnp.swapaxes(weight, 1, 2) for weight in (self_qkv[0], cross_query, cross_kv[0])))
+    weights = together(*(jnp.swapaxes(weight, 1, 2) for weight in (self_qkv[0], cross_kv[0])))
     weights = lax.all_gather(weights, "mp", axis=0)
+    mp_index, x_index = lax.axis_index("mp"), lax.axis_index("pairs") % MP
+    quarter = lax.dynamic_slice_in_dim(jnp.swapaxes(cross_query[0], 0, 1), x_index * (COLS // MP), COLS // MP)
+    quarters = jnp.stack([quarter] + [from_mp(quarter, apart) for apart in APART[1:]])
     spread = lax.all_to_all(
         embed(enc_tokens, embed_weight, side_index), "pairs", split_axis=0, concat_axis=0, tiled=True
     )
+    spread, quarters = lax.optimization_barrier((spread, quarters))
+    slices = [quarters] + [from_x(quarters, apart) for apart in APART[1:]]
     views = enc_tokens.shape[0]
     taken = views // 2
     own = spread.reshape((-1,) + spread.shape[2:])
@@ -305,9 +365,11 @@
     slots = jnp.where(within // taken == side_index, slots, slots + own.shape[0])
     packets = pick(slots, own, other)
     pieces = lax.all_to_all(packets, ("pairs", "mp"), split_axis=0, concat_axis=0, tiled=True)
+    pieces, slices = lax.optimization_barrier((pieces, slices))
     partner = lax.ppermute(pieces, "side", flip)
-    after_self = self_block(pieces, weights, self_out[0], norm_gains[0])
-    final_rows = cross_block(after_self, partner, weights, cross_out[0], norm_gains[0])
+    after_self, cross_weights = self_block(pieces, weights, self_out[0], norm_gains[0])
+    place = jnp.stack([mp_index, x_index])
+    final_rows = cross_block(place, after_self, partner, slices, cross_weights, cross_out[0], norm_gains[0])
     final_rows = lax.all_to_all(
         final_rows.reshape(MP, TOK // MP, D), "mp", split_axis=0, concat_axis=0, tiled=True
     )

time: 142 us -> 136 us (0.958)
  blocking collectives: 85 us -> 15.4 us
  starting transfers between devices: 0.01 us -> 30.5 us
  waiting for transfers between devices: 11.8 us -> 40.1 us
  local copies, waits for them, and re-layouts: 1.29 us -> 5.83 us
    all_to_all x2 -> x0, blocking collectives: 69.1 us -> none  [the longest x1 35 us: local(): lax.all_to_all(packets, ('pairs', 'mp'), split_axis=0, concat_axis=0, til...]
    ppermute x0 -> x6, waiting for transfers between devices: none -> 24.4 us  [the longest x3 18.2 us: from_x(): return lax.ppermute(value, 'pairs', pairs)]
    all_to_all x0 -> x2, starting transfers between devices: none -> 21 us  [the longest x1 11.6 us: local(): lax.all_to_all(embed(enc_tokens, embed_weight, side_index), 'pairs', spli...]
    all_to_all x0 -> x2, waiting for transfers between devices: none -> 11.2 us  [the longest x1 9.91 us: local(): lax.all_to_all(embed(enc_tokens, embed_weight, side_index), 'pairs', spli...]
    ppermute x0 -> x6, starting transfers between devices: none -> 9.49 us  [the longest x3 5.31 us: from_mp(): lax.ppermute(value, 'mp', [((index + apart) % MP, index) for index in ran...]
    all_gather x1, waiting for transfers between devices: 9.41 us -> 2.17 us  [local(): weights = lax.all_gather(weights, 'mp', axis=0)]
    unnamed x10 -> x24, local copies, waits for them, and re-layouts: 1.29 us -> 4.92 us
  transfers between devices with their start and end apart: 3 -> 11, of which waited for: 2 -> 9; matrix products, arithmetic and copies ran while one was open for 0% -> 1% of each run, Pallas kernels for 10% -> 11%
where the time goes in v2:
time: 136 us
  waiting for transfers between devices  40.1 us (29%)
  starting transfers between devices  30.5 us (22%)
  Pallas kernels  28.6 us (21%)
  blocking collectives  15.4 us (11%)
  between operations  13.5 us (10%)
  local copies, waits for them, and re-layouts  5.83 us (4%)
  matrix products  1.95 us (1%)
    ppermute x3, waiting for transfers between devices, from_x(): return lax.ppermute(value, 'pairs', pairs)  18.2 us
    all_to_all x1, blocking collectives, local(): lax.all_to_all(final_rows.reshape(MP, TOK // MP, D), 'mp', split_axis=0,...  15.4 us
    pallas_call x1, Pallas kernels, cross_block(): pl.pallas_call(cross_kernel, out_shape=jax.ShapeDtypeStruct((TOK, D), jnp...  11.6 us
    all_to_all x1, starting transfers between devices, local(): lax.all_to_all(embed(enc_tokens, embed_weight, side_index), 'pairs', spli...  11.6 us
    all_to_all x1, waiting for transfers between devices, local(): lax.all_to_all(embed(enc_tokens, embed_weight, side_index), 'pairs', spli...  9.91 us
    all_to_all x1, starting transfers between devices, local(): lax.all_to_all(packets, ('pairs', 'mp'), split_axis=0, concat_axis=0, til...  9.38 us
    pallas_call x1, Pallas kernels, self_block(): pl.pallas_call(self_kernel, out_shape=(jax.ShapeDtypeStruct((TOK, D), jnp...  9.04 us
    ppermute x3, waiting for transfers between devices, from_mp(): lax.ppermute(value, 'mp', [((index + apart) % MP, index) for index in ran...  6.25 us
  transfers between devices with their start and end apart: 11, of which 9 were waited for; matrix products, arithmetic and copies ran while one was open for 1% of the time, Pallas kernels for 11%

profile of v2, /device:TPU:2, one launch (start us, length us, event | category | flops | bytes accessed | tf_op | source)
XLA Modules:
  0.0 136.0 jit_solution(9935465999741002697)
XLA Ops:
  6.5 0.0 copy-start
  6.5 0.0 all-gather.3.cloned.1.call-start
  6.5 2.3 %together.1 = bf16[5,192,768]{2,1,0:T(8,128)(2,1)} custom-call(bf16[3,192,768]{2,1,0:T(8,128)(2,1)} %bitcast.49, bf16[2,192,768]{2,1,0:T(8,128)(2,1)} %bitcast.50), custom_call_target="tpu_custom_call" | custom-call | bytes 2949120 | tf_op jit(solution)/shard_map/together/pallas_call | solution.py:318
  8.8 0.0 all-gather.3.cloned.1.call-update
  8.9 3.8 %embed.1 = bf16[32,4,8,384]{3,2,1,0:T(8,128)(2,1)} custom-call(s32[1]{0:T(128)} %bitcast.3.side_ref, bf16[8,128,1024]{2,1,0:T(8,128)(2,1)} %tokens_ref.1, bf16[1024,768]{1,0:T(8,128)(2,1)} %weight_ref.1), custom_call_target="tpu_custom_call" | custom-call | flops 805306368 | bytes 3407872 | tf_op jit(solution)/shard_map/embed/pallas_call | solution.py:73
  12.6 0.0 copy-start.11
  12.7 11.6 %all-to-all-start = ((bf16[32,4,8,384]{3,2,1,0:T(8,128)(2,1)}), bf16[32,4,8,384]{3,2,1,0:T(8,128)(2,1)S(1)}, u32[]{:S(2)}, u32[]{:S(2)}) async-start(bf16[32,4,8,384]{3,2,1,0:T(8,128)(2,1)} %embed.1), calls=%async_computation | async-start | bytes 1572864 | tf_op jit(solution)/shard_map/all_to_all | solution.py:353
  24.3 0.9 dynamic-slice_bitcast_fusion
  25.2 3.3 %collective-permute-start.2 = (bf16[48,768]{1,0:T(8,128)(2,1)S(1)}, bf16[48,768]{1,0:T(8,128)(2,1)S(1)}, u32[]{:S(2)}, u32[]{:S(2)}) collective-permute-start(bf16[48,768]{1,0:T(8,128)(2,1)S(1)} %get-tuple-element.24), channel_id=1, source_target_pairs={{2,0},{3,1},{0,2},{1,3},{6,4},{7,5},{4,6},{5,7},{10,8},{11,9},{8,1... | collective-permute-start | bytes 221192 | tf_op jit(solution)/shard_map/ppermute | solution.py:289
  28.5 1.1 collective-permute-start.1
  29.6 1.0 collective-permute-start
  30.5 2.5 %collective-permute-done.2 = bf16[48,768]{1,0:T(8,128)(2,1)S(1)} collective-permute-done((bf16[48,768]{1,0:T(8,128)(2,1)S(1)}, bf16[48,768]{1,0:T(8,128)(2,1)S(1)}, u32[]{:S(2)}, u32[]{:S(2)}) %collective-permute-start.2) | collective-permute-done | bytes 73760 | tf_op jit(solution)/shard_map/ppermute | solution.py:289
  33.0 3.3 %collective-permute-done.1 = bf16[48,768]{1,0:T(8,128)(2,1)S(1)} collective-permute-done((bf16[48,768]{1,0:T(8,128)(2,1)S(1)}, bf16[48,768]{1,0:T(8,128)(2,1)S(1)}, u32[]{:S(2)}, u32[]{:S(2)}) %collective-permute-start.1) | collective-permute-done | bytes 73760 | tf_op jit(solution)/shard_map/ppermute | solution.py:289
  36.4 0.4 collective-permute-done
  36.8 9.9 %all-to-all-done = bf16[32,4,8,384]{3,2,1,0:T(8,128)(2,1)S(1)} async-done(((bf16[32,4,8,384]{3,2,1,0:T(8,128)(2,1)}), bf16[32,4,8,384]{3,2,1,0:T(8,128)(2,1)S(1)}, u32[]{:S(2)}, u32[]{:S(2)}) %all-to-all-start) | async-done | bytes 786464 | tf_op jit(solution)/shard_map/all_to_all | solution.py:353
  46.7 0.0 collective-permute-start.3
  46.7 0.0 copy-done.11
  46.8 0.0 copy-start.9
  46.8 2.2 %collective-permute-done.3.other_ref = bf16[128,8,384]{2,1,0:T(8,128)(2,1)S(1)} collective-permute-done((bf16[128,8,384]{2,1,0:T(8,128)(2,1)S(1)}, bf16[128,8,384]{2,1,0:T(8,128)(2,1)S(1)}, u32[]{:S(2)}, u32[]{:S(2)}) %collective-permute-start.3) | collective-permute-done | bytes 786464 | tf_op jit(solution)/shard_map/ppermute | solution.py:361
  49.0 1.8 %pick.1 = bf16[128,8,384]{2,1,0:T(8,128)(2,1)} custom-call(s32[128]{0:T(128)S(1)} %compare_select_fusion.slots_ref, bf16[128,8,384]{2,1,0:T(8,128)(2,1)S(1)} %bitcast.43, bf16[128,8,384]{2,1,0:T(8,128)(2,1)S(1)} %collective-permute-done.3.other_ref), custom_call_target="tpu_custom_call" | custom-call | flops 393216 | bytes 2359296 | tf_op jit(solution)/shard_map/pick/pallas_call | solution.py:104
  50.9 9.4 %all-to-all-start.1 = ((bf16[128,8,384]{2,1,0:T(8,128)(2,1)}), bf16[128,8,384]{2,1,0:T(8,128)(2,1)S(1)}, u32[]{:S(2)}, u32[]{:S(2)}) async-start(bf16[128,8,384]{2,1,0:T(8,128)(2,1)} %pick.1), calls=%async_computation.1 | async-start | bytes 1572864 | tf_op jit(solution)/shard_map/all_to_all | solution.py:367
  60.3 1.5 %collective-permute-start.4 = (bf16[4,48,768]{2,1,0:T(8,128)(2,1)S(1)}, bf16[4,48,768]{2,1,0:T(8,128)(2,1)S(1)}, u32[]{:S(2)}, u32[]{:S(2)}) collective-permute-start(bf16[4,48,768]{2,1,0:T(8,128)(2,1)S(1)} %pad_maximum_fusion.slices0_ref), channel_id=1, source_target_pairs={{24,0},{0,8},{8,16},{16,24},{56,32},{32,40},{40,48},{48,56},{88,64... | collective-permute-start | bytes 884744 | tf_op jit(solution)/shard_map/ppermute | solution.py:295
  61.8 0.6 collective-permute-start.5
  62.4 2.1 %collective-permute-start.6 = (bf16[4,48,768]{2,1,0:T(8,128)(2,1)S(1)}, bf16[4,48,768]{2,1,0:T(8,128)(2,1)S(1)}, u32[]{:S(2)}, u32[]{:S(2)}) collective-permute-start(bf16[4,48,768]{2,1,0:T(8,128)(2,1)S(1)} %pad_maximum_fusion.slices0_ref), channel_id=1, source_target_pairs={{16,0},{24,8},{0,16},{8,24},{48,32},{56,40},{32,48},{40,56},{80,64... | collective-permute-start | bytes 884744 | tf_op jit(solution)/shard_map/ppermute | solution.py:295
  64.4 10.9 %collective-permute-done.4.slices1_ref = bf16[4,48,768]{2,1,0:T(8,128)(2,1)S(1)} collective-permute-done((bf16[4,48,768]{2,1,0:T(8,128)(2,1)S(1)}, bf16[4,48,768]{2,1,0:T(8,128)(2,1)S(1)}, u32[]{:S(2)}, u32[]{:S(2)}) %collective-permute-start.4) | collective-permute-done | bytes 294944 | tf_op jit(solution)/shard_map/ppermute | solution.py:295
  75.3 0.7 copy-done.3
  76.0 0.0 collective-permute-done.5.slices2_ref
  76.0 0.7 copy-done.5
  76.8 7.3 %collective-permute-done.6.slices3_ref = bf16[4,48,768]{2,1,0:T(8,128)(2,1)S(1)} collective-permute-done((bf16[4,48,768]{2,1,0:T(8,128)(2,1)S(1)}, bf16[4,48,768]{2,1,0:T(8,128)(2,1)S(1)}, u32[]{:S(2)}, u32[]{:S(2)}) %collective-permute-start.6) | collective-permute-done | bytes 294944 | tf_op jit(solution)/shard_map/ppermute | solution.py:295
  84.1 0.7 copy-done.7
  84.8 1.3 all-to-all-done.1.pieces_ref
  86.1 0.0 collective-permute-start.7
  86.1 0.1 pad_add_fusion.place_ref
  86.2 2.2 %all-gather.3.cloned.1.call-done = bf16[20,192,768]{2,1,0:T(8,128)(2,1)} async-done(((bf16[5,192,768]{2,1,0:T(8,128)(2,1)}), bf16[20,192,768]{2,1,0:T(8,128)(2,1)}) %all-gather.3.cloned.1.call-update) | async-done | bytes 5898256 | tf_op jit(solution)/shard_map/all_gather | solution.py:349
  88.3 0.0 copy-done.9
  88.4 1.3 copy-done.1
  89.6 9.0 %self_block.1 = (f32[512,768]{1,0:T(8,128)S(1)}, bf16[4,2,192,768]{3,2,1,0:T(8,128)(2,1)S(1)}) custom-call(bf16[128,8,384]{2,1,0:T(8,128)(2,1)S(1)} %all-to-all-done.1.pieces_ref, bf16[4,5,192,768]{3,2,1,0:T(8,128)(2,1)} %bitcast.54, bf16[768,768]{1,0:T(8,128)(2,1)S(1)} %bitcast.45, f32[4,768]{1,0:T(4,128)S(1)} %bitcast.47), custom_call_target="tpu_custom_call" | custom-call | flops 3221225472 | bytes 8388608 | tf_op jit(solution)/shard_map/self_block/pallas_call | solution.py:257
  98.7 0.0 copy-start.10
  98.7 1.4 %copy-done.10 = bf16[4,2,192,768]{3,2,1,0:T(8,128)(2,1)} copy-done((bf16[4,2,192,768]{3,2,1,0:T(8,128)(2,1)}, bf16[4,2,192,768]{3,2,1,0:T(8,128)(2,1)S(1)}, u32[]{:S(2)}) %copy-start.10) | copy-done | bytes 2359320
  100.1 0.0 collective-permute-done.7.pieces_ref
  100.1 0.0 copy-done.2
  100.1 0.0 copy-done.4
  100.1 0.0 copy-done.6
  100.1 0.0 copy-done.8
  100.1 11.6 %cross_block.1 = bf16[512,768]{1,0:T(8,128)(2,1)S(1)} custom-call(s32[2]{0:T(128)S(1)} %pad_add_fusion.place_ref, f32[512,768]{1,0:T(8,128)S(1)} %get-tuple-element.17.after_ref, bf16[128,8,384]{2,1,0:T(8,128)(2,1)S(1)} %collective-permute-done.7.pieces_ref, bf16[4,48,768]{2,1,0:T(8,128)(2,1)S(1)} %pad_maximum_fusion.slices0_ref, ...), custom_call_target="tpu_custom_call" | custom-call | flops 3221225472 | bytes 8388608 | tf_op jit(solution)/shard_map/cross_block/pallas_call | solution.py:274
  111.8 15.4 %all_to_all.15 = bf16[4,128,768]{2,1,0:T(8,128)(2,1)S(1)} all-to-all(bf16[4,128,768]{2,1,0:T(8,128)(2,1)S(1)} %bitcast.44), channel_id=1, replica_groups=mesh['pairs'=32,'side'=2,'mp'=4] {'mp'}, dimensions={0} | all-to-all | bytes 1572864 | tf_op jit(solution)/shard_map/all_to_all | solution.py:373
  127.2 0.0 copy-done
  127.2 2.0 %fusion.5 = bf16[4,1,128,1024]{3,2,1,0:T(8,128)(2,1)} fusion(bf16[4,128,768]{2,1,0:T(8,128)(2,1)S(1)} %all_to_all.15, bf16[1,768,1024]{2,1,0:T(8,128)(2,1)S(1)} %copy-done), kind=kOutput, calls=%fused_computation.3 | convolution fusion | flops 805830656 | bytes 3407872 | tf_op jit(solution)/shard_map/prd,de->pre/dot_general | solution.py:376
  (10 shorter events, 0.1 us)
Async XLA Ops:
  6.5 120.7 %copy-start = (bf16[1,768,1024]{2,1,0:T(8,128)(2,1)S(1)}, bf16[1,768,1024]{2,1,0:T(8,128)(2,1)}, u32[]{:S(2)}) copy-start(bf16[1,768,1024]{2,1,0:T(8,128)(2,1)} %param.19) | copy-start | bytes 4718596
  6.5 81.8 %all-gather.3.cloned.1.call-start = ((), (), s32[]{:S(2)}) async-start(), calls=%async_computation.3 | async-start | bytes 7372800 | tf_op jit(solution)/shard_map/all_gather | solution.py:349
  12.6 34.1 %copy-start.11 = (s32[128,2]{0,1:T(2,128)S(1)}, s32[128,2]{0,1:T(2,128)}, u32[]{:S(2)}) copy-start(s32[128,2]{0,1:T(2,128)} %param.11) | copy-start | bytes 3076
  12.7 34.1 %all-to-all-start = ((bf16[32,4,8,384]{3,2,1,0:T(8,128)(2,1)}), bf16[32,4,8,384]{3,2,1,0:T(8,128)(2,1)S(1)}, u32[]{:S(2)}, u32[]{:S(2)}) async-start(bf16[32,4,8,384]{3,2,1,0:T(8,128)(2,1)} %embed.1), calls=%async_computation | async-start | bytes 1572864 | tf_op jit(solution)/shard_map/all_to_all | solution.py:353
  25.2 7.8 %collective-permute-start.2 = (bf16[48,768]{1,0:T(8,128)(2,1)S(1)}, bf16[48,768]{1,0:T(8,128)(2,1)S(1)}, u32[]{:S(2)}, u32[]{:S(2)}) collective-permute-start(bf16[48,768]{1,0:T(8,128)(2,1)S(1)} %get-tuple-element.24), channel_id=1, source_target_pairs={{2,0},{3,1},{0,2},{1,3},{6,4},{7,5},{4,6},{5,7},{10,8},{11,9},{8,1... | collective-permute-start | bytes 221192 | tf_op jit(solution)/shard_map/ppermute | solution.py:289
  28.5 7.8 %collective-permute-start.1 = (bf16[48,768]{1,0:T(8,128)(2,1)S(1)}, bf16[48,768]{1,0:T(8,128)(2,1)S(1)}, u32[]{:S(2)}, u32[]{:S(2)}) collective-permute-start(bf16[48,768]{1,0:T(8,128)(2,1)S(1)} %get-tuple-element.24), channel_id=1, source_target_pairs={{1,0},{2,1},{3,2},{0,3},{5,4},{6,5},{7,6},{4,7},{9,8},{10,9},{11,1... | collective-permute-start | bytes 221192 | tf_op jit(solution)/shard_map/ppermute | solution.py:289
  29.6 7.2 %collective-permute-start = (bf16[48,768]{1,0:T(8,128)(2,1)S(1)}, bf16[48,768]{1,0:T(8,128)(2,1)S(1)}, u32[]{:S(2)}, u32[]{:S(2)}) collective-permute-start(bf16[48,768]{1,0:T(8,128)(2,1)S(1)} %get-tuple-element.24), channel_id=1, source_target_pairs={{3,0},{0,1},{1,2},{2,3},{7,4},{4,5},{5,6},{6,7},{11,8},{8,9},{9,10... | collective-permute-start | bytes 221192 | tf_op jit(solution)/shard_map/ppermute | solution.py:289
  46.7 2.3 %collective-permute-start.3 = (bf16[128,8,384]{2,1,0:T(8,128)(2,1)S(1)}, bf16[128,8,384]{2,1,0:T(8,128)(2,1)S(1)}, u32[]{:S(2)}, u32[]{:S(2)}) collective-permute-start(bf16[128,8,384]{2,1,0:T(8,128)(2,1)S(1)} %bitcast.42), channel_id=1, source_target_pairs={{0,4},{4,0},{1,5},{5,1},{2,6},{6,2},{3,7},{7,3},{8,12},{12,8},{9,1... | collective-permute-start | bytes 2359304 | tf_op jit(solution)/shard_map/ppermute | solution.py:361
  46.8 41.6 %copy-start.9 = (f32[1,4,768]{2,1,0:T(4,128)S(1)}, f32[1,4,768]{2,1,0:T(4,128)}, u32[]{:S(2)}) copy-start(f32[1,4,768]{2,1,0:T(4,128)} %param.18) | copy-start | bytes 36868
  50.9 35.2 %all-to-all-start.1 = ((bf16[128,8,384]{2,1,0:T(8,128)(2,1)}), bf16[128,8,384]{2,1,0:T(8,128)(2,1)S(1)}, u32[]{:S(2)}, u32[]{:S(2)}) async-start(bf16[128,8,384]{2,1,0:T(8,128)(2,1)} %pick.1), calls=%async_computation.1 | async-start | bytes 1572864 | tf_op jit(solution)/shard_map/all_to_all | solution.py:367
  60.3 15.1 %collective-permute-start.4 = (bf16[4,48,768]{2,1,0:T(8,128)(2,1)S(1)}, bf16[4,48,768]{2,1,0:T(8,128)(2,1)S(1)}, u32[]{:S(2)}, u32[]{:S(2)}) collective-permute-start(bf16[4,48,768]{2,1,0:T(8,128)(2,1)S(1)} %pad_maximum_fusion.slices0_ref), channel_id=1, source_target_pairs={{24,0},{0,8},{8,16},{16,24},{56,32},{32,40},{40,48},{48,56},{88,64... | collective-permute-start | bytes 884744 | tf_op jit(solution)/shard_map/ppermute | solution.py:295
  61.8 14.2 %collective-permute-start.5 = (bf16[4,48,768]{2,1,0:T(8,128)(2,1)S(1)}, bf16[4,48,768]{2,1,0:T(8,128)(2,1)S(1)}, u32[]{:S(2)}, u32[]{:S(2)}) collective-permute-start(bf16[4,48,768]{2,1,0:T(8,128)(2,1)S(1)} %pad_maximum_fusion.slices0_ref), channel_id=1, source_target_pairs={{8,0},{16,8},{24,16},{0,24},{40,32},{48,40},{56,48},{32,56},{72,64... | collective-permute-start | bytes 884744 | tf_op jit(solution)/shard_map/ppermute | solution.py:295
  62.4 21.7 %collective-permute-start.6 = (bf16[4,48,768]{2,1,0:T(8,128)(2,1)S(1)}, bf16[4,48,768]{2,1,0:T(8,128)(2,1)S(1)}, u32[]{:S(2)}, u32[]{:S(2)}) collective-permute-start(bf16[4,48,768]{2,1,0:T(8,128)(2,1)S(1)} %pad_maximum_fusion.slices0_ref), channel_id=1, source_target_pairs={{16,0},{24,8},{0,16},{8,24},{48,32},{56,40},{32,48},{40,56},{80,64... | collective-permute-start | bytes 884744 | tf_op jit(solution)/shard_map/ppermute | solution.py:295
  75.3 0.7 copy-start.3
  76.0 0.7 copy-start.5
  84.1 0.7 copy-start.7
  86.1 14.0 %collective-permute-start.7 = (bf16[128,8,384]{2,1,0:T(8,128)(2,1)S(1)}, bf16[128,8,384]{2,1,0:T(8,128)(2,1)S(1)}, u32[]{:S(2)}, u32[]{:S(2)}) collective-permute-start(bf16[128,8,384]{2,1,0:T(8,128)(2,1)S(1)} %all-to-all-done.1.pieces_ref), channel_id=1, source_target_pairs={{0,4},{4,0},{1,5},{5,1},{2,6},{6,2},{3,7},{7,3},{8,12},{12,8},{9,1... | collective-permute-start | bytes 2359304 | tf_op jit(solution)/shard_map/ppermute | solution.py:369
  88.4 1.3 copy-start.1
  89.6 10.5 %copy-start.2 = (bf16[1,768,768]{2,1,0:T(8,128)(2,1)S(1)}, bf16[1,768,768]{2,1,0:T(8,128)(2,1)}, u32[]{:S(2)}) copy-start(bf16[1,768,768]{2,1,0:T(8,128)(2,1)} %param.17) | copy-start | bytes 3538948
  89.6 10.5 %copy-start.4 = (bf16[4,48,768]{2,1,0:T(8,128)(2,1)S(1)}, bf16[4,48,768]{2,1,0:T(8,128)(2,1)}, u32[]{:S(2)}) copy-start(bf16[4,48,768]{2,1,0:T(8,128)(2,1)} %copy-done.3) | copy-start | bytes 884740
  89.6 10.5 %copy-start.6 = (bf16[4,48,768]{2,1,0:T(8,128)(2,1)S(1)}, bf16[4,48,768]{2,1,0:T(8,128)(2,1)}, u32[]{:S(2)}) copy-start(bf16[4,48,768]{2,1,0:T(8,128)(2,1)} %copy-done.5) | copy-start | bytes 884740
  89.6 10.5 %copy-start.8 = (bf16[4,48,768]{2,1,0:T(8,128)(2,1)S(1)}, bf16[4,48,768]{2,1,0:T(8,128)(2,1)}, u32[]{:S(2)}) copy-start(bf16[4,48,768]{2,1,0:T(8,128)(2,1)} %copy-done.7) | copy-start | bytes 884740
  98.7 1.4 %copy-start.10 = (bf16[4,2,192,768]{3,2,1,0:T(8,128)(2,1)}, bf16[4,2,192,768]{3,2,1,0:T(8,128)(2,1)S(1)}, u32[]{:S(2)}) copy-start(bf16[4,2,192,768]{3,2,1,0:T(8,128)(2,1)S(1)} %get-tuple-element.22.weight_ref) | copy-start | bytes 7077892
Sparse Core Ops, SparseCore 0:
  9.2 79.1 all-gather.2

commit v3 on v2

--- a/solution.py
+++ b/solution.py
@@ -189,45 +189,51 @@
             attended_ref[top : top + CHUNK, quad * WINDOW : (quad + 1) * WINDOW] = mixture.astype(jnp.bfloat16)
 
 
+def fetch(gathered_ref, first_kind, weight_ref, sems):
+    kinds = weight_ref.shape[1]
+    waiting = []
+    for owner in range(MP):
+        source = gathered_ref.at[owner, first_kind : first_kind + kinds]
+        waiting.append(pltpu.make_async_copy(source, weight_ref.at[owner], sems.at[owner]))
+        waiting[owner].start()
+
+    def ready(quad):
+        last = ((quad + 1) * WINDOW - 1) // COLS
+        while waiting and MP - len(waiting) <= last:
+            waiting.pop(0).wait()
+
+    return ready
+
+
 def self_kernel(
-    pieces_ref, gathered_ref, out_weight_ref, gain_ref, out_ref, cross_ref, normed_ref, attended_ref, weight_ref, sems
+    pieces_ref, gathered_ref, out_weight_ref, gain_ref, out_ref, normed_ref, attended_ref, weight_ref, sems
 ):
-    fetched = []
-    for owner in range(MP):
-        fetched.append(
-            pltpu.make_async_copy(gathered_ref.at[owner, 0:KINDS], weight_ref.at[owner], sems.at[owner])
-        )
-        fetched[owner].start()
-    passed = pltpu.make_async_copy(gathered_ref.at[:, KINDS:], cross_ref, sems.at[MP])
-    passed.start()
+    ready = fetch(gathered_ref, 0, weight_ref, sems)
     unpack(pieces_ref, out_ref)
     normalise(out_ref, gain_ref[0:1], normed_ref)
     normed = normed_ref[...]
-    waited = []
 
     def quad_of(quad):
-        while len(waited) <= (quad * WINDOW + WINDOW - 1) // COLS:
-            fetched[len(waited)].wait()
-            waited.append(True)
+        ready(quad)
         return [project(normed, of_kind(weight_ref, kind), quad) for kind in range(KINDS)]
 
     attend(quad_of, attended_ref)
     out_ref[...] += jnp.dot(attended_ref[...], out_weight_ref[...], preferred_element_type=jnp.float32)
-    passed.wait()
 
 
 def cross_kernel(
-    place_ref, after_ref, pieces_ref, slices0_ref, slices1_ref, slices2_ref, slices3_ref, weight_ref, out_weight_ref,
-    gain_ref, out_ref, rows_ref, query_ref, partner_ref, attended_ref, slices_ref, sems,
+    place_ref, after_ref, pieces_ref, slices0_ref, slices1_ref, slices2_ref, slices3_ref, gathered_ref, out_weight_ref,
+    gain_ref, out_ref, rows_ref, query_ref, partner_ref, attended_ref, slices_ref, weight_ref, slice_sems, sems,
 ):
     fetched = []
     for count, source in enumerate((slices0_ref, slices1_ref, slices2_ref, slices3_ref)):
         along_x = lax.rem(place_ref[1] + APART[count], MP)
         for place in range(MP):
             owner = lax.rem(place_ref[0] + APART[place], MP)
-            sem = sems.at[count * MP + place]
+            sem = slice_sems.at[count * MP + place]
             fetched.append(pltpu.make_async_copy(source.at[place], slices_ref.at[owner, along_x], sem))
             fetched[-1].start()
+    ready = fetch(gathered_ref, KINDS, weight_ref, sems)
     unpack(pieces_ref, rows_ref)
     normalise(rows_ref, gain_ref[2:3], partner_ref)
     normalise(after_ref, gain_ref[1:2], query_ref)
@@ -238,14 +244,15 @@
     def query_columns(owner, first, last):
         return slices_ref[owner].reshape(COLS, D)[first:last]
 
-    attend(
-        lambda quad: (
+    def quad_of(quad):
+        ready(quad)
+        return (
             project(queries, query_columns, quad),
             project(partner, of_kind(weight_ref, 0), quad),
             project(partner, of_kind(weight_ref, 1), quad),
-        ),
-        attended_ref,
-    )
+        )
+
+    attend(quad_of, attended_ref)
     rows_ref[...] = after_ref[...] + jnp.dot(
         attended_ref[...], out_weight_ref[...], preferred_element_type=jnp.float32
     )
@@ -253,17 +260,13 @@
 
 
 def self_block(pieces, weights, out_weight, gains):
-    rest = weights.shape[1] - KINDS
     return pl.pallas_call(
         self_kernel,
-        out_shape=(
-            jax.ShapeDtypeStruct((TOK, D), jnp.float32),
-            jax.ShapeDtypeStruct((MP, rest, COLS, D), jnp.bfloat16),
-        ),
+        out_shape=jax.ShapeDtypeStruct((TOK, D), jnp.float32),
         in_specs=in_vmem(1) + in_hbm(1) + in_vmem(2),
-        out_specs=tuple(in_vmem(2)),
+        out_specs=in_vmem(1)[0],
         scratch_shapes=[pltpu.VMEM((TOK, D), jnp.bfloat16)] * 2
-        + [pltpu.VMEM((MP, KINDS, COLS, D), jnp.bfloat16), pltpu.SemaphoreType.DMA((MP + 1,))],
+        + [pltpu.VMEM((MP, KINDS, COLS, D), jnp.bfloat16), pltpu.SemaphoreType.DMA((MP,))],
         compiler_params=pltpu.CompilerParams(vmem_limit_bytes=VMEM),
         cost_estimate=estimate(8 * TOK * D * D + 4 * TOK * TOK * D, 8 * 2**20, HEADS * TOK * TOK),
         name="self_block",
@@ -271,14 +274,20 @@
 
 
 def cross_block(place, after_self, pieces, slices, weights, out_weight, gains):
+    kinds = weights.shape[1] - KINDS
     return pl.pallas_call(
         cross_kernel,
         out_shape=jax.ShapeDtypeStruct((TOK, D), jnp.bfloat16),
-        in_specs=[pl.BlockSpec(memory_space=pltpu.SMEM)] + in_vmem(2) + in_hbm(MP) + in_vmem(3),
+        in_specs=[pl.BlockSpec(memory_space=pltpu.SMEM)] + in_vmem(2) + in_hbm(MP + 1) + in_vmem(2),
         out_specs=in_vmem(1)[0],
         scratch_shapes=[pltpu.VMEM((TOK, D), jnp.float32)]
         + [pltpu.VMEM((TOK, D), jnp.bfloat16)] * 3
-        + [pltpu.VMEM((MP,) + slices[0].shape, jnp.bfloat16), pltpu.SemaphoreType.DMA((MP * MP,))],
+        + [
+            pltpu.VMEM((MP,) + slices[0].shape, jnp.bfloat16),
+            pltpu.VMEM((MP, kinds, COLS, D), jnp.bfloat16),
+            pltpu.SemaphoreType.DMA((MP * MP,)),
+            pltpu.SemaphoreType.DMA((MP,)),
+        ],
         compiler_params=pltpu.CompilerParams(vmem_limit_bytes=VMEM),
         cost_estimate=estimate(8 * TOK * D * D + 4 * TOK * TOK * D, 8 * 2**20, HEADS * TOK * TOK),
         name="cross_block",
@@ -367,9 +376,9 @@
     pieces = lax.all_to_all(packets, ("pairs", "mp"), split_axis=0, concat_axis=0, tiled=True)
     pieces, slices = lax.optimization_barrier((pieces, slices))
     partner = lax.ppermute(pieces, "side", flip)
-    after_self, cross_weights = self_block(pieces, weights, self_out[0], norm_gains[0])
+    after_self = self_block(pieces, weights, self_out[0], norm_gains[0])
     place = jnp.stack([mp_index, x_index])
-    final_rows = cross_block(place, after_self, partner, slices, cross_weights, cross_out[0], norm_gains[0])
+    final_rows = cross_block(place, after_self, partner, slices, weights, cross_out[0], norm_gains[0])
     final_rows = lax.all_to_all(
         final_rows.reshape(MP, TOK // MP, D), "mp", split_axis=0, concat_axis=0, tiled=True
     )

time: 136 us -> 135 us (level)
  local copies, waits for them, and re-layouts: 5.83 us -> 4.41 us
    unnamed x24 -> x22, local copies, waits for them, and re-layouts: 4.92 us -> 3.49 us
where the time goes in v3:
time: 135 us; the launch traced here: 134 us
  waiting for transfers between devices  40.5 us (30%)
  starting transfers between devices  30.5 us (23%)
  Pallas kernels  28.6 us (21%)
  blocking collectives  14.9 us (11%)
  between operations  13.5 us (10%)
  local copies, waits for them, and re-layouts  4.41 us (3%)
  matrix products  1.95 us (1%)
    ppermute x3, waiting for transfers between devices, from_x(): return lax.ppermute(value, 'pairs', pairs)  18.5 us
    all_to_all x1, blocking collectives, local(): lax.all_to_all(final_rows.reshape(MP, TOK // MP, D), 'mp', split_axis=0,...  14.9 us
    pallas_call x1, Pallas kernels, cross_block(): pl.pallas_call(cross_kernel, out_shape=jax.ShapeDtypeStruct((TOK, D), jnp...  11.6 us
    all_to_all x1, starting transfers between devices, local(): lax.all_to_all(embed(enc_tokens, embed_weight, side_index), 'pairs', spli...  11.6 us
    all_to_all x1, starting transfers between devices, local(): lax.all_to_all(packets, ('pairs', 'mp'), split_axis=0, concat_axis=0, til...  9.38 us
    all_to_all x1, waiting for transfers between devices, local(): lax.all_to_all(embed(enc_tokens, embed_weight, side_index), 'pairs', spli...  9.07 us
    pallas_call x1, Pallas kernels, self_block(): pl.pallas_call(self_kernel, out_shape=jax.ShapeDtypeStruct((TOK, D), jnp....  9.02 us
    ppermute x3, waiting for transfers between devices, from_mp(): lax.ppermute(value, 'mp', [((index + apart) % MP, index) for index in ran...  7.1 us
  transfers between devices with their start and end apart: 11, of which 9 were waited for; matrix products, arithmetic and copies ran while one was open for 1% of the time, Pallas kernels for 11%

profile of v3, /device:TPU:2, one launch (start us, length us, event | category | flops | bytes accessed | tf_op | source)
XLA Modules:
  0.0 134.5 jit_solution(9413076964564673600)
XLA Ops:
  6.5 0.0 copy-start
  6.5 0.0 all-gather.3.cloned.1.call-start
  6.5 2.3 %together.1 = bf16[5,192,768]{2,1,0:T(8,128)(2,1)} custom-call(bf16[3,192,768]{2,1,0:T(8,128)(2,1)} %bitcast.49, bf16[2,192,768]{2,1,0:T(8,128)(2,1)} %bitcast.50), custom_call_target="tpu_custom_call" | custom-call | bytes 2949120 | tf_op jit(solution)/shard_map/together/pallas_call | solution.py:327
  8.8 0.0 all-gather.3.cloned.1.call-update
  8.9 3.8 %embed.1 = bf16[32,4,8,384]{3,2,1,0:T(8,128)(2,1)} custom-call(s32[1]{0:T(128)} %bitcast.3.side_ref, bf16[8,128,1024]{2,1,0:T(8,128)(2,1)} %tokens_ref.1, bf16[1024,768]{1,0:T(8,128)(2,1)} %weight_ref.1), custom_call_target="tpu_custom_call" | custom-call | flops 805306368 | bytes 3407872 | tf_op jit(solution)/shard_map/embed/pallas_call | solution.py:73
  12.6 0.0 copy-start.10
  12.7 11.6 %all-to-all-start = ((bf16[32,4,8,384]{3,2,1,0:T(8,128)(2,1)}), bf16[32,4,8,384]{3,2,1,0:T(8,128)(2,1)S(1)}, u32[]{:S(2)}, u32[]{:S(2)}) async-start(bf16[32,4,8,384]{3,2,1,0:T(8,128)(2,1)} %embed.1), calls=%async_computation | async-start | bytes 1572864 | tf_op jit(solution)/shard_map/all_to_all | solution.py:362
  24.3 0.9 dynamic-slice_bitcast_fusion
  25.2 3.1 %collective-permute-start.1 = (bf16[48,768]{1,0:T(8,128)(2,1)S(1)}, bf16[48,768]{1,0:T(8,128)(2,1)S(1)}, u32[]{:S(2)}, u32[]{:S(2)}) collective-permute-start(bf16[48,768]{1,0:T(8,128)(2,1)S(1)} %get-tuple-element.20), channel_id=1, source_target_pairs={{1,0},{2,1},{3,2},{0,3},{5,4},{6,5},{7,6},{4,7},{9,8},{10,9},{11,1... | collective-permute-start | bytes 221192 | tf_op jit(solution)/shard_map/ppermute | solution.py:298
  28.3 0.0 collective-permute-start
  28.3 2.2 %collective-permute-start.2 = (bf16[48,768]{1,0:T(8,128)(2,1)S(1)}, bf16[48,768]{1,0:T(8,128)(2,1)S(1)}, u32[]{:S(2)}, u32[]{:S(2)}) collective-permute-start(bf16[48,768]{1,0:T(8,128)(2,1)S(1)} %get-tuple-element.20), channel_id=1, source_target_pairs={{2,0},{3,1},{0,2},{1,3},{6,4},{7,5},{4,6},{5,7},{10,8},{11,9},{8,1... | collective-permute-start | bytes 221192 | tf_op jit(solution)/shard_map/ppermute | solution.py:298
  30.5 1.3 collective-permute-done.1
  31.8 4.8 %collective-permute-done = bf16[48,768]{1,0:T(8,128)(2,1)S(1)} collective-permute-done((bf16[48,768]{1,0:T(8,128)(2,1)S(1)}, bf16[48,768]{1,0:T(8,128)(2,1)S(1)}, u32[]{:S(2)}, u32[]{:S(2)}) %collective-permute-start) | collective-permute-done | bytes 73760 | tf_op jit(solution)/shard_map/ppermute | solution.py:298
  36.6 1.0 collective-permute-done.2
  37.7 9.1 %all-to-all-done = bf16[32,4,8,384]{3,2,1,0:T(8,128)(2,1)S(1)} async-done(((bf16[32,4,8,384]{3,2,1,0:T(8,128)(2,1)}), bf16[32,4,8,384]{3,2,1,0:T(8,128)(2,1)S(1)}, u32[]{:S(2)}, u32[]{:S(2)}) %all-to-all-start) | async-done | bytes 786464 | tf_op jit(solution)/shard_map/all_to_all | solution.py:362
  46.7 0.0 collective-permute-start.3
  46.7 0.0 copy-done.10
  46.8 0.0 copy-start.9
  46.8 2.2 %collective-permute-done.3.other_ref = bf16[128,8,384]{2,1,0:T(8,128)(2,1)S(1)} collective-permute-done((bf16[128,8,384]{2,1,0:T(8,128)(2,1)S(1)}, bf16[128,8,384]{2,1,0:T(8,128)(2,1)S(1)}, u32[]{:S(2)}, u32[]{:S(2)}) %collective-permute-start.3) | collective-permute-done | bytes 786464 | tf_op jit(solution)/shard_map/ppermute | solution.py:370
  49.0 1.8 %pick.1 = bf16[128,8,384]{2,1,0:T(8,128)(2,1)} custom-call(s32[128]{0:T(128)S(1)} %compare_select_fusion.slots_ref, bf16[128,8,384]{2,1,0:T(8,128)(2,1)S(1)} %bitcast.43, bf16[128,8,384]{2,1,0:T(8,128)(2,1)S(1)} %collective-permute-done.3.other_ref), custom_call_target="tpu_custom_call" | custom-call | flops 393216 | bytes 2359296 | tf_op jit(solution)/shard_map/pick/pallas_call | solution.py:104
  50.9 9.4 %all-to-all-start.1 = ((bf16[128,8,384]{2,1,0:T(8,128)(2,1)}), bf16[128,8,384]{2,1,0:T(8,128)(2,1)S(1)}, u32[]{:S(2)}, u32[]{:S(2)}) async-start(bf16[128,8,384]{2,1,0:T(8,128)(2,1)} %pick.1), calls=%async_computation.1 | async-start | bytes 1572864 | tf_op jit(solution)/shard_map/all_to_all | solution.py:376
  60.3 2.2 %collective-permute-start.6 = (bf16[4,48,768]{2,1,0:T(8,128)(2,1)S(1)}, bf16[4,48,768]{2,1,0:T(8,128)(2,1)S(1)}, u32[]{:S(2)}, u32[]{:S(2)}) collective-permute-start(bf16[4,48,768]{2,1,0:T(8,128)(2,1)S(1)} %pad_maximum_fusion.slices0_ref), channel_id=1, source_target_pairs={{16,0},{24,8},{0,16},{8,24},{48,32},{56,40},{32,48},{40,56},{80,64... | collective-permute-start | bytes 884744 | tf_op jit(solution)/shard_map/ppermute | solution.py:304
  62.4 1.5 %collective-permute-start.5 = (bf16[4,48,768]{2,1,0:T(8,128)(2,1)S(1)}, bf16[4,48,768]{2,1,0:T(8,128)(2,1)S(1)}, u32[]{:S(2)}, u32[]{:S(2)}) collective-permute-start(bf16[4,48,768]{2,1,0:T(8,128)(2,1)S(1)} %pad_maximum_fusion.slices0_ref), channel_id=1, source_target_pairs={{8,0},{16,8},{24,16},{0,24},{40,32},{48,40},{56,48},{32,56},{72,64... | collective-permute-start | bytes 884744 | tf_op jit(solution)/shard_map/ppermute | solution.py:304
  63.9 0.6 collective-permute-start.4
  64.4 12.3 %collective-permute-done.6.slices3_ref = bf16[4,48,768]{2,1,0:T(8,128)(2,1)S(1)} collective-permute-done((bf16[4,48,768]{2,1,0:T(8,128)(2,1)S(1)}, bf16[4,48,768]{2,1,0:T(8,128)(2,1)S(1)}, u32[]{:S(2)}, u32[]{:S(2)}) %collective-permute-start.6) | collective-permute-done | bytes 294944 | tf_op jit(solution)/shard_map/ppermute | solution.py:304
  76.7 0.0 copy-start.3
  76.7 0.7 copy-done.3
  77.5 6.2 %collective-permute-done.5.slices2_ref = bf16[4,48,768]{2,1,0:T(8,128)(2,1)S(1)} collective-permute-done((bf16[4,48,768]{2,1,0:T(8,128)(2,1)S(1)}, bf16[4,48,768]{2,1,0:T(8,128)(2,1)S(1)}, u32[]{:S(2)}, u32[]{:S(2)}) %collective-permute-start.5) | collective-permute-done | bytes 294944 | tf_op jit(solution)/shard_map/ppermute | solution.py:304
  83.6 0.0 copy-start.5
  83.6 0.7 copy-done.5
  84.4 0.0 collective-permute-done.4.slices1_ref
  84.4 0.7 copy-done.7
  85.1 1.0 all-to-all-done.1.pieces_ref
  86.1 0.0 collective-permute-start.7
  86.1 0.1 pad_add_fusion.place_ref
  86.2 2.6 %all-gather.3.cloned.1.call-done = bf16[20,192,768]{2,1,0:T(8,128)(2,1)} async-done(((bf16[5,192,768]{2,1,0:T(8,128)(2,1)}), bf16[20,192,768]{2,1,0:T(8,128)(2,1)}) %all-gather.3.cloned.1.call-update) | async-done | bytes 5898256 | tf_op jit(solution)/shard_map/all_gather | solution.py:358
  88.7 0.0 copy-done.9
  88.8 1.3 copy-done.1
  90.0 9.0 %self_block.1.after_ref = f32[512,768]{1,0:T(8,128)S(1)} custom-call(bf16[128,8,384]{2,1,0:T(8,128)(2,1)S(1)} %all-to-all-done.1.pieces_ref, bf16[4,5,192,768]{3,2,1,0:T(8,128)(2,1)} %bitcast.54, bf16[768,768]{1,0:T(8,128)(2,1)S(1)} %bitcast.45, f32[4,768]{1,0:T(4,128)S(1)} %bitcast.47), custom_call_target="tpu_custom_call" | custom-call | flops 3221225472 | bytes 8388608 | tf_op jit(solution)/shard_map/self_block/pallas_call | solution.py:263
  99.1 0.0 collective-permute-done.7.pieces_ref
  99.1 0.0 copy-done.2
  99.1 0.0 copy-done.4
  99.1 0.0 copy-done.6
  99.1 0.0 copy-done.8
  99.1 11.6 %cross_block.1 = bf16[512,768]{1,0:T(8,128)(2,1)S(1)} custom-call(s32[2]{0:T(128)S(1)} %pad_add_fusion.place_ref, f32[512,768]{1,0:T(8,128)S(1)} %self_block.1.after_ref, bf16[128,8,384]{2,1,0:T(8,128)(2,1)S(1)} %collective-permute-done.7.pieces_ref, bf16[4,48,768]{2,1,0:T(8,128)(2,1)S(1)} %pad_maximum_fusion.slices0_ref, bf16[4,48,768]{2,1,0:T(8,128)(2,1)S(1)} %copy-done.8, ...), custom_call_target="tpu_custom_call" | custom-call | flops 3221225472 | bytes 8388608 | tf_op jit(solution)/shard_map/cross_block/pallas_call | solution.py:278
  110.8 14.9 %all_to_all.15 = bf16[4,128,768]{2,1,0:T(8,128)(2,1)S(1)} all-to-all(bf16[4,128,768]{2,1,0:T(8,128)(2,1)S(1)} %bitcast.44), channel_id=1, replica_groups=mesh['pairs'=32,'side'=2,'mp'=4] {'mp'}, dimensions={0} | all-to-all | bytes 1572864 | tf_op jit(solution)/shard_map/all_to_all | solution.py:382
  125.7 0.0 copy-done
  125.7 2.0 %fusion.5 = bf16[4,1,128,1024]{3,2,1,0:T(8,128)(2,1)} fusion(bf16[4,128,768]{2,1,0:T(8,128)(2,1)S(1)} %all_to_all.15, bf16[1,768,1024]{2,1,0:T(8,128)(2,1)S(1)} %copy-done), kind=kOutput, calls=%fused_computation.3 | convolution fusion | flops 805830656 | bytes 3407872 | tf_op jit(solution)/shard_map/prd,de->pre/dot_general | solution.py:385
  (8 shorter events, 0.1 us)
Async XLA Ops:
  6.5 119.2 %copy-start = (bf16[1,768,1024]{2,1,0:T(8,128)(2,1)S(1)}, bf16[1,768,1024]{2,1,0:T(8,128)(2,1)}, u32[]{:S(2)}) copy-start(bf16[1,768,1024]{2,1,0:T(8,128)(2,1)} %param.19) | copy-start | bytes 4718596
  6.5 82.2 %all-gather.3.cloned.1.call-start = ((), (), s32[]{:S(2)}) async-start(), calls=%async_computation.3 | async-start | bytes 7372800 | tf_op jit(solution)/shard_map/all_gather | solution.py:358
  12.6 34.1 %copy-start.10 = (s32[128,2]{0,1:T(2,128)S(1)}, s32[128,2]{0,1:T(2,128)}, u32[]{:S(2)}) copy-start(s32[128,2]{0,1:T(2,128)} %param.11) | copy-start | bytes 3076
  12.7 34.1 %all-to-all-start = ((bf16[32,4,8,384]{3,2,1,0:T(8,128)(2,1)}), bf16[32,4,8,384]{3,2,1,0:T(8,128)(2,1)S(1)}, u32[]{:S(2)}, u32[]{:S(2)}) async-start(bf16[32,4,8,384]{3,2,1,0:T(8,128)(2,1)} %embed.1), calls=%async_computation | async-start | bytes 1572864 | tf_op jit(solution)/shard_map/all_to_all | solution.py:362
  25.2 6.6 %collective-permute-start.1 = (bf16[48,768]{1,0:T(8,128)(2,1)S(1)}, bf16[48,768]{1,0:T(8,128)(2,1)S(1)}, u32[]{:S(2)}, u32[]{:S(2)}) collective-permute-start(bf16[48,768]{1,0:T(8,128)(2,1)S(1)} %get-tuple-element.20), channel_id=1, source_target_pairs={{1,0},{2,1},{3,2},{0,3},{5,4},{6,5},{7,6},{4,7},{9,8},{10,9},{11,1... | collective-permute-start | bytes 221192 | tf_op jit(solution)/shard_map/ppermute | solution.py:298
  28.3 8.3 %collective-permute-start = (bf16[48,768]{1,0:T(8,128)(2,1)S(1)}, bf16[48,768]{1,0:T(8,128)(2,1)S(1)}, u32[]{:S(2)}, u32[]{:S(2)}) collective-permute-start(bf16[48,768]{1,0:T(8,128)(2,1)S(1)} %get-tuple-element.20), channel_id=1, source_target_pairs={{3,0},{0,1},{1,2},{2,3},{7,4},{4,5},{5,6},{6,7},{11,8},{8,9},{9,10... | collective-permute-start | bytes 221192 | tf_op jit(solution)/shard_map/ppermute | solution.py:298
  28.3 9.3 %collective-permute-start.2 = (bf16[48,768]{1,0:T(8,128)(2,1)S(1)}, bf16[48,768]{1,0:T(8,128)(2,1)S(1)}, u32[]{:S(2)}, u32[]{:S(2)}) collective-permute-start(bf16[48,768]{1,0:T(8,128)(2,1)S(1)} %get-tuple-element.20), channel_id=1, source_target_pairs={{2,0},{3,1},{0,2},{1,3},{6,4},{7,5},{4,6},{5,7},{10,8},{11,9},{8,1... | collective-permute-start | bytes 221192 | tf_op jit(solution)/shard_map/ppermute | solution.py:298
  46.7 2.3 %collective-permute-start.3 = (bf16[128,8,384]{2,1,0:T(8,128)(2,1)S(1)}, bf16[128,8,384]{2,1,0:T(8,128)(2,1)S(1)}, u32[]{:S(2)}, u32[]{:S(2)}) collective-permute-start(bf16[128,8,384]{2,1,0:T(8,128)(2,1)S(1)} %bitcast.42), channel_id=1, source_target_pairs={{0,4},{4,0},{1,5},{5,1},{2,6},{6,2},{3,7},{7,3},{8,12},{12,8},{9,1... | collective-permute-start | bytes 2359304 | tf_op jit(solution)/shard_map/ppermute | solution.py:370
  46.8 42.0 %copy-start.9 = (f32[1,4,768]{2,1,0:T(4,128)S(1)}, f32[1,4,768]{2,1,0:T(4,128)}, u32[]{:S(2)}) copy-start(f32[1,4,768]{2,1,0:T(4,128)} %param.18) | copy-start | bytes 36868
  50.9 35.2 %all-to-all-start.1 = ((bf16[128,8,384]{2,1,0:T(8,128)(2,1)}), bf16[128,8,384]{2,1,0:T(8,128)(2,1)S(1)}, u32[]{:S(2)}, u32[]{:S(2)}) async-start(bf16[128,8,384]{2,1,0:T(8,128)(2,1)} %pick.1), calls=%async_computation.1 | async-start | bytes 1572864 | tf_op jit(solution)/shard_map/all_to_all | solution.py:376
  60.3 16.5 %collective-permute-start.6 = (bf16[4,48,768]{2,1,0:T(8,128)(2,1)S(1)}, bf16[4,48,768]{2,1,0:T(8,128)(2,1)S(1)}, u32[]{:S(2)}, u32[]{:S(2)}) collective-permute-start(bf16[4,48,768]{2,1,0:T(8,128)(2,1)S(1)} %pad_maximum_fusion.slices0_ref), channel_id=1, source_target_pairs={{16,0},{24,8},{0,16},{8,24},{48,32},{56,40},{32,48},{40,56},{80,64... | collective-permute-start | bytes 884744 | tf_op jit(solution)/shard_map/ppermute | solution.py:304
  62.4 21.2 %collective-permute-start.5 = (bf16[4,48,768]{2,1,0:T(8,128)(2,1)S(1)}, bf16[4,48,768]{2,1,0:T(8,128)(2,1)S(1)}, u32[]{:S(2)}, u32[]{:S(2)}) collective-permute-start(bf16[4,48,768]{2,1,0:T(8,128)(2,1)S(1)} %pad_maximum_fusion.slices0_ref), channel_id=1, source_target_pairs={{8,0},{16,8},{24,16},{0,24},{40,32},{48,40},{56,48},{32,56},{72,64... | collective-permute-start | bytes 884744 | tf_op jit(solution)/shard_map/ppermute | solution.py:304
  63.9 20.5 %collective-permute-start.4 = (bf16[4,48,768]{2,1,0:T(8,128)(2,1)S(1)}, bf16[4,48,768]{2,1,0:T(8,128)(2,1)S(1)}, u32[]{:S(2)}, u32[]{:S(2)}) collective-permute-start(bf16[4,48,768]{2,1,0:T(8,128)(2,1)S(1)} %pad_maximum_fusion.slices0_ref), channel_id=1, source_target_pairs={{24,0},{0,8},{8,16},{16,24},{56,32},{32,40},{40,48},{48,56},{88,64... | collective-permute-start | bytes 884744 | tf_op jit(solution)/shard_map/ppermute | solution.py:304
  76.7 0.7 copy-start.3
  83.6 0.7 copy-start.5
  84.4 0.7 copy-start.7
  86.1 13.0 %collective-permute-start.7 = (bf16[128,8,384]{2,1,0:T(8,128)(2,1)S(1)}, bf16[128,8,384]{2,1,0:T(8,128)(2,1)S(1)}, u32[]{:S(2)}, u32[]{:S(2)}) collective-permute-start(bf16[128,8,384]{2,1,0:T(8,128)(2,1)S(1)} %all-to-all-done.1.pieces_ref), channel_id=1, source_target_pairs={{0,4},{4,0},{1,5},{5,1},{2,6},{6,2},{3,7},{7,3},{8,12},{12,8},{9,1... | collective-permute-start | bytes 2359304 | tf_op jit(solution)/shard_map/ppermute | solution.py:378
  88.8 1.3 copy-start.1
  90.0 9.1 %copy-start.2 = (bf16[1,768,768]{2,1,0:T(8,128)(2,1)S(1)}, bf16[1,768,768]{2,1,0:T(8,128)(2,1)}, u32[]{:S(2)}) copy-start(bf16[1,768,768]{2,1,0:T(8,128)(2,1)} %param.17) | copy-start | bytes 3538948
  90.0 9.1 %copy-start.4 = (bf16[4,48,768]{2,1,0:T(8,128)(2,1)S(1)}, bf16[4,48,768]{2,1,0:T(8,128)(2,1)}, u32[]{:S(2)}) copy-start(bf16[4,48,768]{2,1,0:T(8,128)(2,1)} %copy-done.3) | copy-start | bytes 884740
  90.0 9.1 %copy-start.6 = (bf16[4,48,768]{2,1,0:T(8,128)(2,1)S(1)}, bf16[4,48,768]{2,1,0:T(8,128)(2,1)}, u32[]{:S(2)}) copy-start(bf16[4,48,768]{2,1,0:T(8,128)(2,1)} %copy-done.5) | copy-start | bytes 884740
  90.0 9.1 %copy-start.8 = (bf16[4,48,768]{2,1,0:T(8,128)(2,1)S(1)}, bf16[4,48,768]{2,1,0:T(8,128)(2,1)}, u32[]{:S(2)}) copy-start(bf16[4,48,768]{2,1,0:T(8,128)(2,1)} %copy-done.7) | copy-start | bytes 884740
Sparse Core Ops, SparseCore 0:
  9.2 79.5 all-gather.2

commit v4 on v3

--- a/solution.py
+++ b/solution.py
@@ -16,7 +16,6 @@
 PIECE_ROWS = 8
 PIECE_COLS = 384
 HALVES = D // PIECE_COLS
-APART = (0, -1 % MP, 1, 2)
 CHUNK = 512
 AHEAD = 1
 LOG_SCALE = 1.4426950408889634 * HEAD_DIM**-0.5
@@ -227,12 +226,9 @@
 ):
     fetched = []
     for count, source in enumerate((slices0_ref, slices1_ref, slices2_ref, slices3_ref)):
-        along_x = lax.rem(place_ref[1] + APART[count], MP)
-        for place in range(MP):
-            owner = lax.rem(place_ref[0] + APART[place], MP)
-            sem = slice_sems.at[count * MP + place]
-            fetched.append(pltpu.make_async_copy(source.at[place], slices_ref.at[owner, along_x], sem))
-            fetched[-1].start()
+        along_x = lax.rem(place_ref[0] + count, MP)
+        fetched.append(pltpu.make_async_copy(source, slices_ref.at[:, along_x], slice_sems.at[count]))
+        fetched[count].start()
     ready = fetch(gathered_ref, KINDS, weight_ref, sems)
     unpack(pieces_ref, rows_ref)
     normalise(rows_ref, gain_ref[2:3], partner_ref)
@@ -285,7 +281,7 @@
         + [
             pltpu.VMEM((MP,) + slices[0].shape, jnp.bfloat16),
             pltpu.VMEM((MP, kinds, COLS, D), jnp.bfloat16),
-            pltpu.SemaphoreType.DMA((MP * MP,)),
+            pltpu.SemaphoreType.DMA((MP,)),
             pltpu.SemaphoreType.DMA((MP,)),
         ],
         compiler_params=pltpu.CompilerParams(vmem_limit_bytes=VMEM),
@@ -358,12 +354,13 @@
     weights = lax.all_gather(weights, "mp", axis=0)
     mp_index, x_index = lax.axis_index("mp"), lax.axis_index("pairs") % MP
     quarter = lax.dynamic_slice_in_dim(jnp.swapaxes(cross_query[0], 0, 1), x_index * (COLS // MP), COLS // MP)
-    quarters = jnp.stack([quarter] + [from_mp(quarter, apart) for apart in APART[1:]])
+    quarters = [quarter] + [from_mp(quarter, apart) for apart in range(1, MP)]
+    quarters = jnp.stack([lax.select_n((owner - mp_index) % MP, *quarters) for owner in range(MP)])
     spread = lax.all_to_all(
         embed(enc_tokens, embed_weight, side_index), "pairs", split_axis=0, concat_axis=0, tiled=True
     )
     spread, quarters = lax.optimization_barrier((spread, quarters))
-    slices = [quarters] + [from_x(quarters, apart) for apart in APART[1:]]
+    slices = [quarters] + [from_x(quarters, apart) for apart in range(1, MP)]
     views = enc_tokens.shape[0]
     taken = views // 2
     own = spread.reshape((-1,) + spread.shape[2:])
@@ -377,7 +374,7 @@
     pieces, slices = lax.optimization_barrier((pieces, slices))
     partner = lax.ppermute(pieces, "side", flip)
     after_self = self_block(pieces, weights, self_out[0], norm_gains[0])
-    place = jnp.stack([mp_index, x_index])
+    place = x_index.reshape(1)
     final_rows = cross_block(place, after_self, partner, slices, weights, cross_out[0], norm_gains[0])
     final_rows = lax.all_to_all(
         final_rows.reshape(MP, TOK // MP, D), "mp", split_axis=0, concat_axis=0, tiled=True

time: 135 us -> 133 us (0.985)
  Pallas kernels: 28.6 us -> 26.4 us
  starting transfers between devices: 30.5 us -> 32.4 us
  waiting for transfers between devices: 40.5 us -> 38.6 us
    ppermute x3, waiting for transfers between devices: 7.1 us -> 4.15 us  [from_mp(): lax.ppermute(value, 'mp', [((index + apart) % MP, index) for index in ran...]
    all_to_all x1, waiting for transfers between devices: 9.07 us -> 11.6 us  [local(): lax.all_to_all(embed(enc_tokens, embed_weight, side_index), 'pairs', spli...]
    pallas_call x1, Pallas kernels: 11.6 us -> 9.48 us  [cross_block(): pl.pallas_call(cross_kernel, out_shape=jax.ShapeDtypeStruct((TOK, D), jnp...]
    unnamed x22 -> x24, local copies, waits for them, and re-layouts: 3.49 us -> 3.49 us
  transfers between devices with their start and end apart: 11 -> 11, of which waited for: 9 -> 9; matrix products, arithmetic and copies ran while one was open for 1% -> 0% of each run, Pallas kernels for 11% -> 11%
where the time goes in v4:
time: 133 us
  waiting for transfers between devices  38.6 us (29%)
  starting transfers between devices  32.4 us (24%)
  Pallas kernels  26.4 us (20%)
  blocking collectives  15.9 us (12%)
  between operations  13.6 us (10%)
  local copies, waits for them, and re-layouts  3.5 us (3%)
  matrix products  1.95 us (1%)
    ppermute x3, waiting for transfers between devices, from_x(): return lax.ppermute(value, 'pairs', pairs)  18.2 us
    all_to_all x1, blocking collectives, local(): lax.all_to_all(final_rows.reshape(MP, TOK // MP, D), 'mp', split_axis=0,...  15.9 us
    all_to_all x1, starting transfers between devices, local(): lax.all_to_all(embed(enc_tokens, embed_weight, side_index), 'pairs', spli...  11.8 us
    all_to_all x1, waiting for transfers between devices, local(): lax.all_to_all(embed(enc_tokens, embed_weight, side_index), 'pairs', spli...  11.6 us
    pallas_call x1, Pallas kernels, cross_block(): pl.pallas_call(cross_kernel, out_shape=jax.ShapeDtypeStruct((TOK, D), jnp...  9.48 us
    all_to_all x1, starting transfers between devices, local(): lax.all_to_all(packets, ('pairs', 'mp'), split_axis=0, concat_axis=0, til...  9.38 us
    pallas_call x1, Pallas kernels, self_block(): pl.pallas_call(self_kernel, out_shape=jax.ShapeDtypeStruct((TOK, D), jnp....  9.02 us
    ppermute x3, starting transfers between devices, from_mp(): lax.ppermute(value, 'mp', [((index + apart) % MP, index) for index in ran...  6.52 us
  transfers between devices with their start and end apart: 11, of which 9 were waited for; matrix products, arithmetic and copies ran while one was open for 0% of the time, Pallas kernels for 11%

profile of v4, /device:TPU:2, one launch (start us, length us, event | category | flops | bytes accessed | tf_op | source)
XLA Modules:
  0.0 132.5 jit_solution(8007799301902457344)
XLA Ops:
  6.5 0.0 copy-start
  6.5 0.0 all-gather.3.cloned.1.call-start
  6.5 2.3 %together.1 = bf16[5,192,768]{2,1,0:T(8,128)(2,1)} custom-call(bf16[3,192,768]{2,1,0:T(8,128)(2,1)} %bitcast.52, bf16[2,192,768]{2,1,0:T(8,128)(2,1)} %bitcast.53), custom_call_target="tpu_custom_call" | custom-call | bytes 2949120 | tf_op jit(solution)/shard_map/together/pallas_call | solution.py:323
  8.8 0.0 all-gather.3.cloned.1.call-update
  8.9 3.8 %embed.1 = bf16[32,4,8,384]{3,2,1,0:T(8,128)(2,1)} custom-call(s32[1]{0:T(128)} %bitcast.2.side_ref, bf16[8,128,1024]{2,1,0:T(8,128)(2,1)} %tokens_ref.1, bf16[1024,768]{1,0:T(8,128)(2,1)} %weight_ref.1), custom_call_target="tpu_custom_call" | custom-call | flops 805306368 | bytes 3407872 | tf_op jit(solution)/shard_map/embed/pallas_call | solution.py:72
  12.7 0.0 copy-start.10
  12.7 0.0 copy-start.11
  12.7 11.8 %all-to-all-start = ((bf16[32,4,8,384]{3,2,1,0:T(8,128)(2,1)}), bf16[32,4,8,384]{3,2,1,0:T(8,128)(2,1)S(1)}, u32[]{:S(2)}, u32[]{:S(2)}) async-start(bf16[32,4,8,384]{3,2,1,0:T(8,128)(2,1)} %embed.1), calls=%async_computation | async-start | bytes 1572864 | tf_op jit(solution)/shard_map/all_to_all | solution.py:359
  24.5 0.0 copy-done.10
  24.5 3.3 %collective-permute-start.1 = (bf16[48,768]{1,0:T(8,128)(2,1)S(1)}, bf16[48,768]{1,0:T(8,128)(2,1)S(1)}, u32[]{:S(2)}, u32[]{:S(2)}) collective-permute-start(bf16[48,768]{1,0:T(8,128)(2,1)S(1)} %dynamic-slice_bitcast_fusion), channel_id=1, source_target_pairs={{2,0},{3,1},{0,2},{1,3},{6,4},{7,5},{4,6},{5,7},{10,8},{11,9},{8,1... | collective-permute-start | bytes 221192 | tf_op jit(solution)/shard_map/ppermute | solution.py:294
  27.8 0.7 collective-permute-start.2
  28.4 2.6 %collective-permute-start = (bf16[48,768]{1,0:T(8,128)(2,1)S(1)}, bf16[48,768]{1,0:T(8,128)(2,1)S(1)}, u32[]{:S(2)}, u32[]{:S(2)}) collective-permute-start(bf16[48,768]{1,0:T(8,128)(2,1)S(1)} %dynamic-slice_bitcast_fusion), channel_id=1, source_target_pairs={{1,0},{2,1},{3,2},{0,3},{5,4},{6,5},{7,6},{4,7},{9,8},{10,9},{11,1... | collective-permute-start | bytes 221192 | tf_op jit(solution)/shard_map/ppermute | solution.py:294
  31.0 1.8 %collective-permute-done.1 = bf16[48,768]{1,0:T(8,128)(2,1)S(1)} collective-permute-done((bf16[48,768]{1,0:T(8,128)(2,1)S(1)}, bf16[48,768]{1,0:T(8,128)(2,1)S(1)}, u32[]{:S(2)}, u32[]{:S(2)}) %collective-permute-start.1) | collective-permute-done | bytes 73760 | tf_op jit(solution)/shard_map/ppermute | solution.py:294
  32.8 2.4 %collective-permute-done.2 = bf16[48,768]{1,0:T(8,128)(2,1)S(1)} collective-permute-done((bf16[48,768]{1,0:T(8,128)(2,1)S(1)}, bf16[48,768]{1,0:T(8,128)(2,1)S(1)}, u32[]{:S(2)}, u32[]{:S(2)}) %collective-permute-start.2) | collective-permute-done | bytes 73760 | tf_op jit(solution)/shard_map/ppermute | solution.py:294
  35.2 0.0 collective-permute-done
  35.2 0.1 select_bitcast_fusion.3
  35.3 11.6 %all-to-all-done = bf16[32,4,8,384]{3,2,1,0:T(8,128)(2,1)S(1)} async-done(((bf16[32,4,8,384]{3,2,1,0:T(8,128)(2,1)}), bf16[32,4,8,384]{3,2,1,0:T(8,128)(2,1)S(1)}, u32[]{:S(2)}, u32[]{:S(2)}) %all-to-all-start) | async-done | bytes 786464 | tf_op jit(solution)/shard_map/all_to_all | solution.py:359
  46.9 0.0 collective-permute-start.3
  46.9 0.0 copy-done.11
  46.9 0.0 copy-start.9
  46.9 2.2 %collective-permute-done.3.other_ref = bf16[128,8,384]{2,1,0:T(8,128)(2,1)S(1)} collective-permute-done((bf16[128,8,384]{2,1,0:T(8,128)(2,1)S(1)}, bf16[128,8,384]{2,1,0:T(8,128)(2,1)S(1)}, u32[]{:S(2)}, u32[]{:S(2)}) %collective-permute-start.3) | collective-permute-done | bytes 786464 | tf_op jit(solution)/shard_map/ppermute | solution.py:367
  49.2 1.8 %pick.1 = bf16[128,8,384]{2,1,0:T(8,128)(2,1)} custom-call(s32[128]{0:T(128)S(1)} %compare_select_fusion.slots_ref, bf16[128,8,384]{2,1,0:T(8,128)(2,1)S(1)} %bitcast.46, bf16[128,8,384]{2,1,0:T(8,128)(2,1)S(1)} %collective-permute-done.3.other_ref), custom_call_target="tpu_custom_call" | custom-call | flops 393216 | bytes 2359296 | tf_op jit(solution)/shard_map/pick/pallas_call | solution.py:103
  51.0 9.4 %all-to-all-start.1 = ((bf16[128,8,384]{2,1,0:T(8,128)(2,1)}), bf16[128,8,384]{2,1,0:T(8,128)(2,1)S(1)}, u32[]{:S(2)}, u32[]{:S(2)}) async-start(bf16[128,8,384]{2,1,0:T(8,128)(2,1)} %pick.1), calls=%async_computation.1 | async-start | bytes 1572864 | tf_op jit(solution)/shard_map/all_to_all | solution.py:373
  60.4 1.5 %collective-permute-start.6 = (bf16[4,48,768]{2,1,0:T(8,128)(2,1)S(1)}, bf16[4,48,768]{2,1,0:T(8,128)(2,1)S(1)}, u32[]{:S(2)}, u32[]{:S(2)}) collective-permute-start(bf16[4,48,768]{2,1,0:T(8,128)(2,1)S(1)} %pad_maximum_fusion.slices0_ref), channel_id=1, source_target_pairs={{24,0},{0,8},{8,16},{16,24},{56,32},{32,40},{40,48},{48,56},{88,64... | collective-permute-start | bytes 884744 | tf_op jit(solution)/shard_map/ppermute | solution.py:300
  62.0 1.5 %collective-permute-start.5 = (bf16[4,48,768]{2,1,0:T(8,128)(2,1)S(1)}, bf16[4,48,768]{2,1,0:T(8,128)(2,1)S(1)}, u32[]{:S(2)}, u32[]{:S(2)}) collective-permute-start(bf16[4,48,768]{2,1,0:T(8,128)(2,1)S(1)} %pad_maximum_fusion.slices0_ref), channel_id=1, source_target_pairs={{16,0},{24,8},{0,16},{8,24},{48,32},{56,40},{32,48},{40,56},{80,64... | collective-permute-start | bytes 884744 | tf_op jit(solution)/shard_map/ppermute | solution.py:300
  63.4 1.7 %collective-permute-start.4 = (bf16[4,48,768]{2,1,0:T(8,128)(2,1)S(1)}, bf16[4,48,768]{2,1,0:T(8,128)(2,1)S(1)}, u32[]{:S(2)}, u32[]{:S(2)}) collective-permute-start(bf16[4,48,768]{2,1,0:T(8,128)(2,1)S(1)} %pad_maximum_fusion.slices0_ref), channel_id=1, source_target_pairs={{8,0},{16,8},{24,16},{0,24},{40,32},{48,40},{56,48},{32,56},{72,64... | collective-permute-start | bytes 884744 | tf_op jit(solution)/shard_map/ppermute | solution.py:300
  65.2 10.3 %collective-permute-done.6.slices3_ref = bf16[4,48,768]{2,1,0:T(8,128)(2,1)S(1)} collective-permute-done((bf16[4,48,768]{2,1,0:T(8,128)(2,1)S(1)}, bf16[4,48,768]{2,1,0:T(8,128)(2,1)S(1)}, u32[]{:S(2)}, u32[]{:S(2)}) %collective-permute-start.6) | collective-permute-done | bytes 294944 | tf_op jit(solution)/shard_map/ppermute | solution.py:300
  75.5 0.0 copy-start.3
  75.5 0.7 copy-done.3
  76.2 2.8 %collective-permute-done.5.slices2_ref = bf16[4,48,768]{2,1,0:T(8,128)(2,1)S(1)} collective-permute-done((bf16[4,48,768]{2,1,0:T(8,128)(2,1)S(1)}, bf16[4,48,768]{2,1,0:T(8,128)(2,1)S(1)}, u32[]{:S(2)}, u32[]{:S(2)}) %collective-permute-start.5) | collective-permute-done | bytes 294944 | tf_op jit(solution)/shard_map/ppermute | solution.py:300
  79.1 0.7 copy-done.5
  79.8 5.1 %collective-permute-done.4.slices1_ref = bf16[4,48,768]{2,1,0:T(8,128)(2,1)S(1)} collective-permute-done((bf16[4,48,768]{2,1,0:T(8,128)(2,1)S(1)}, bf16[4,48,768]{2,1,0:T(8,128)(2,1)S(1)}, u32[]{:S(2)}, u32[]{:S(2)}) %collective-permute-start.4) | collective-permute-done | bytes 294944 | tf_op jit(solution)/shard_map/ppermute | solution.py:300
  84.8 0.7 copy-done.7
  85.6 0.7 all-to-all-done.1.pieces_ref
  86.2 0.0 collective-permute-start.7
  86.2 1.7 %all-gather.3.cloned.1.call-done = bf16[20,192,768]{2,1,0:T(8,128)(2,1)} async-done(((bf16[5,192,768]{2,1,0:T(8,128)(2,1)}), bf16[20,192,768]{2,1,0:T(8,128)(2,1)}) %all-gather.3.cloned.1.call-update) | async-done | bytes 5898256 | tf_op jit(solution)/shard_map/all_gather | solution.py:354
  88.0 0.0 copy-done.9
  88.0 1.3 copy-done.1
  89.2 9.0 %self_block.1.after_ref = f32[512,768]{1,0:T(8,128)S(1)} custom-call(bf16[128,8,384]{2,1,0:T(8,128)(2,1)S(1)} %all-to-all-done.1.pieces_ref, bf16[4,5,192,768]{3,2,1,0:T(8,128)(2,1)} %bitcast.54, bf16[768,768]{1,0:T(8,128)(2,1)S(1)} %bitcast.48, f32[4,768]{1,0:T(4,128)S(1)} %bitcast.50), custom_call_target="tpu_custom_call" | custom-call | flops 3221225472 | bytes 8388608 | tf_op jit(solution)/shard_map/self_block/pallas_call | solution.py:259
  98.3 0.0 collective-permute-done.7.pieces_ref
  98.3 0.0 copy-done.2
  98.3 0.0 copy-done.4
  98.3 0.0 copy-done.6
  98.3 0.0 copy-done.8
  98.3 9.5 %cross_block.1 = bf16[512,768]{1,0:T(8,128)(2,1)S(1)} custom-call(s32[1]{0:T(128)} %bitcast.place_ref, f32[512,768]{1,0:T(8,128)S(1)} %self_block.1.after_ref, bf16[128,8,384]{2,1,0:T(8,128)(2,1)S(1)} %collective-permute-done.7.pieces_ref, bf16[4,48,768]{2,1,0:T(8,128)(2,1)S(1)} %pad_maximum_fusion.slices0_ref, bf16[4,48,768]{2,1,0:T(8,128)(2,1)S(1)} %copy-done.8, ...), custom_call_target="tpu_custom_call" | custom-call | flops 3221225472 | bytes 8388608 | tf_op jit(solution)/shard_map/cross_block/pallas_call | solution.py:274
  107.8 15.9 %all_to_all.15 = bf16[4,128,768]{2,1,0:T(8,128)(2,1)S(1)} all-to-all(bf16[4,128,768]{2,1,0:T(8,128)(2,1)S(1)} %bitcast.47), channel_id=1, replica_groups=mesh['pairs'=32,'side'=2,'mp'=4] {'mp'}, dimensions={0} | all-to-all | bytes 1572864 | tf_op jit(solution)/shard_map/all_to_all | solution.py:379
  123.7 0.0 copy-done
  123.7 2.0 %fusion.5 = bf16[4,1,128,1024]{3,2,1,0:T(8,128)(2,1)} fusion(bf16[4,128,768]{2,1,0:T(8,128)(2,1)S(1)} %all_to_all.15, bf16[1,768,1024]{2,1,0:T(8,128)(2,1)S(1)} %copy-done), kind=kOutput, calls=%fused_computation.3 | convolution fusion | flops 805830656 | bytes 3407872 | tf_op jit(solution)/shard_map/prd,de->pre/dot_general | solution.py:382
  (10 shorter events, 0.1 us)
Async XLA Ops:
  6.5 117.2 %copy-start = (bf16[1,768,1024]{2,1,0:T(8,128)(2,1)S(1)}, bf16[1,768,1024]{2,1,0:T(8,128)(2,1)}, u32[]{:S(2)}) copy-start(bf16[1,768,1024]{2,1,0:T(8,128)(2,1)} %param.19) | copy-start | bytes 4718596
  6.5 81.4 %all-gather.3.cloned.1.call-start = ((), (), s32[]{:S(2)}) async-start(), calls=%async_computation.3 | async-start | bytes 7372800 | tf_op jit(solution)/shard_map/all_gather | solution.py:354
  12.7 11.8 %copy-start.10 = (bf16[1,768,192]{1,2,0:T(8,128)(2,1)S(1)}, bf16[1,768,192]{1,2,0:T(8,128)(2,1)}, u32[]{:S(2)}) copy-start(bf16[1,768,192]{1,2,0:T(8,128)(2,1)} %param.15) | copy-start | bytes 884740
  12.7 34.2 %copy-start.11 = (s32[128,2]{0,1:T(2,128)S(1)}, s32[128,2]{0,1:T(2,128)}, u32[]{:S(2)}) copy-start(s32[128,2]{0,1:T(2,128)} %param.11) | copy-start | bytes 3076
  12.7 34.2 %all-to-all-start = ((bf16[32,4,8,384]{3,2,1,0:T(8,128)(2,1)}), bf16[32,4,8,384]{3,2,1,0:T(8,128)(2,1)S(1)}, u32[]{:S(2)}, u32[]{:S(2)}) async-start(bf16[32,4,8,384]{3,2,1,0:T(8,128)(2,1)} %embed.1), calls=%async_computation | async-start | bytes 1572864 | tf_op jit(solution)/shard_map/all_to_all | solution.py:359
  24.5 8.3 %collective-permute-start.1 = (bf16[48,768]{1,0:T(8,128)(2,1)S(1)}, bf16[48,768]{1,0:T(8,128)(2,1)S(1)}, u32[]{:S(2)}, u32[]{:S(2)}) collective-permute-start(bf16[48,768]{1,0:T(8,128)(2,1)S(1)} %dynamic-slice_bitcast_fusion), channel_id=1, source_target_pairs={{2,0},{3,1},{0,2},{1,3},{6,4},{7,5},{4,6},{5,7},{10,8},{11,9},{8,1... | collective-permute-start | bytes 221192 | tf_op jit(solution)/shard_map/ppermute | solution.py:294
  27.8 7.4 %collective-permute-start.2 = (bf16[48,768]{1,0:T(8,128)(2,1)S(1)}, bf16[48,768]{1,0:T(8,128)(2,1)S(1)}, u32[]{:S(2)}, u32[]{:S(2)}) collective-permute-start(bf16[48,768]{1,0:T(8,128)(2,1)S(1)} %dynamic-slice_bitcast_fusion), channel_id=1, source_target_pairs={{3,0},{0,1},{1,2},{2,3},{7,4},{4,5},{5,6},{6,7},{11,8},{8,9},{9,10... | collective-permute-start | bytes 221192 | tf_op jit(solution)/shard_map/ppermute | solution.py:294
  28.4 6.7 %collective-permute-start = (bf16[48,768]{1,0:T(8,128)(2,1)S(1)}, bf16[48,768]{1,0:T(8,128)(2,1)S(1)}, u32[]{:S(2)}, u32[]{:S(2)}) collective-permute-start(bf16[48,768]{1,0:T(8,128)(2,1)S(1)} %dynamic-slice_bitcast_fusion), channel_id=1, source_target_pairs={{1,0},{2,1},{3,2},{0,3},{5,4},{6,5},{7,6},{4,7},{9,8},{10,9},{11,1... | collective-permute-start | bytes 221192 | tf_op jit(solution)/shard_map/ppermute | solution.py:294
  46.9 2.3 %collective-permute-start.3 = (bf16[128,8,384]{2,1,0:T(8,128)(2,1)S(1)}, bf16[128,8,384]{2,1,0:T(8,128)(2,1)S(1)}, u32[]{:S(2)}, u32[]{:S(2)}) collective-permute-start(bf16[128,8,384]{2,1,0:T(8,128)(2,1)S(1)} %bitcast.45), channel_id=1, source_target_pairs={{0,4},{4,0},{1,5},{5,1},{2,6},{6,2},{3,7},{7,3},{8,12},{12,8},{9,1... | collective-permute-start | bytes 2359304 | tf_op jit(solution)/shard_map/ppermute | solution.py:367
  46.9 41.0 %copy-start.9 = (f32[1,4,768]{2,1,0:T(4,128)S(1)}, f32[1,4,768]{2,1,0:T(4,128)}, u32[]{:S(2)}) copy-start(f32[1,4,768]{2,1,0:T(4,128)} %param.18) | copy-start | bytes 36868
  51.0 35.2 %all-to-all-start.1 = ((bf16[128,8,384]{2,1,0:T(8,128)(2,1)}), bf16[128,8,384]{2,1,0:T(8,128)(2,1)S(1)}, u32[]{:S(2)}, u32[]{:S(2)}) async-start(bf16[128,8,384]{2,1,0:T(8,128)(2,1)} %pick.1), calls=%async_computation.1 | async-start | bytes 1572864 | tf_op jit(solution)/shard_map/all_to_all | solution.py:373
  60.4 15.1 %collective-permute-start.6 = (bf16[4,48,768]{2,1,0:T(8,128)(2,1)S(1)}, bf16[4,48,768]{2,1,0:T(8,128)(2,1)S(1)}, u32[]{:S(2)}, u32[]{:S(2)}) collective-permute-start(bf16[4,48,768]{2,1,0:T(8,128)(2,1)S(1)} %pad_maximum_fusion.slices0_ref), channel_id=1, source_target_pairs={{24,0},{0,8},{8,16},{16,24},{56,32},{32,40},{40,48},{48,56},{88,64... | collective-permute-start | bytes 884744 | tf_op jit(solution)/shard_map/ppermute | solution.py:300
  62.0 17.1 %collective-permute-start.5 = (bf16[4,48,768]{2,1,0:T(8,128)(2,1)S(1)}, bf16[4,48,768]{2,1,0:T(8,128)(2,1)S(1)}, u32[]{:S(2)}, u32[]{:S(2)}) collective-permute-start(bf16[4,48,768]{2,1,0:T(8,128)(2,1)S(1)} %pad_maximum_fusion.slices0_ref), channel_id=1, source_target_pairs={{16,0},{24,8},{0,16},{8,24},{48,32},{56,40},{32,48},{40,56},{80,64... | collective-permute-start | bytes 884744 | tf_op jit(solution)/shard_map/ppermute | solution.py:300
  63.4 21.4 %collective-permute-start.4 = (bf16[4,48,768]{2,1,0:T(8,128)(2,1)S(1)}, bf16[4,48,768]{2,1,0:T(8,128)(2,1)S(1)}, u32[]{:S(2)}, u32[]{:S(2)}) collective-permute-start(bf16[4,48,768]{2,1,0:T(8,128)(2,1)S(1)} %pad_maximum_fusion.slices0_ref), channel_id=1, source_target_pairs={{8,0},{16,8},{24,16},{0,24},{40,32},{48,40},{56,48},{32,56},{72,64... | collective-permute-start | bytes 884744 | tf_op jit(solution)/shard_map/ppermute | solution.py:300
  75.5 0.7 copy-start.3
  79.1 0.7 copy-start.5
  84.8 0.7 copy-start.7
  86.2 12.0 %collective-permute-start.7 = (bf16[128,8,384]{2,1,0:T(8,128)(2,1)S(1)}, bf16[128,8,384]{2,1,0:T(8,128)(2,1)S(1)}, u32[]{:S(2)}, u32[]{:S(2)}) collective-permute-start(bf16[128,8,384]{2,1,0:T(8,128)(2,1)S(1)} %all-to-all-done.1.pieces_ref), channel_id=1, source_target_pairs={{0,4},{4,0},{1,5},{5,1},{2,6},{6,2},{3,7},{7,3},{8,12},{12,8},{9,1... | collective-permute-start | bytes 2359304 | tf_op jit(solution)/shard_map/ppermute | solution.py:375
  88.0 1.3 copy-start.1
  89.2 9.1 %copy-start.2 = (bf16[1,768,768]{2,1,0:T(8,128)(2,1)S(1)}, bf16[1,768,768]{2,1,0:T(8,128)(2,1)}, u32[]{:S(2)}) copy-start(bf16[1,768,768]{2,1,0:T(8,128)(2,1)} %param.17) | copy-start | bytes 3538948
  89.2 9.1 %copy-start.4 = (bf16[4,48,768]{2,1,0:T(8,128)(2,1)S(1)}, bf16[4,48,768]{2,1,0:T(8,128)(2,1)}, u32[]{:S(2)}) copy-start(bf16[4,48,768]{2,1,0:T(8,128)(2,1)} %copy-done.3) | copy-start | bytes 884740
  89.2 9.1 %copy-start.6 = (bf16[4,48,768]{2,1,0:T(8,128)(2,1)S(1)}, bf16[4,48,768]{2,1,0:T(8,128)(2,1)}, u32[]{:S(2)}) copy-start(bf16[4,48,768]{2,1,0:T(8,128)(2,1)} %copy-done.5) | copy-start | bytes 884740
  89.2 9.1 %copy-start.8 = (bf16[4,48,768]{2,1,0:T(8,128)(2,1)S(1)}, bf16[4,48,768]{2,1,0:T(8,128)(2,1)}, u32[]{:S(2)}) copy-start(bf16[4,48,768]{2,1,0:T(8,128)(2,1)} %copy-done.7) | copy-start | bytes 884740
Sparse Core Ops, SparseCore 0:
  9.2 78.7 all-gather.2

commit v5 on v4

--- a/solution.py
+++ b/solution.py
@@ -95,7 +95,7 @@
         out_ref[pair] = jnp.where(foreign, other_ref[slot], own_ref[slot])
         return carry
 
-    lax.fori_loop(0, out_ref.shape[0], step, 0, unroll=8)
+    lax.fori_loop(0, out_ref.shape[0], step, 0, unroll=32)
 
 
 def pick(slots, own, other):

time: 133 us -> 133 us (level)
  no operation moved by 1% of the time
where the time goes in v5:
time: 133 us
  waiting for transfers between devices  38.6 us (29%)
  starting transfers between devices  32.4 us (24%)
  Pallas kernels  26.3 us (20%)
  blocking collectives  15.9 us (12%)
  between operations  13.6 us (10%)
  local copies, waits for them, and re-layouts  3.5 us (3%)
  matrix products  1.95 us (1%)
    ppermute x3, waiting for transfers between devices, from_x(): return lax.ppermute(value, 'pairs', pairs)  18.2 us
    all_to_all x1, blocking collectives, local(): lax.all_to_all(final_rows.reshape(MP, TOK // MP, D), 'mp', split_axis=0,...  15.9 us
    all_to_all x1, starting transfers between devices, local(): lax.all_to_all(embed(enc_tokens, embed_weight, side_index), 'pairs', spli...  11.8 us
    all_to_all x1, waiting for transfers between devices, local(): lax.all_to_all(embed(enc_tokens, embed_weight, side_index), 'pairs', spli...  11.6 us
    pallas_call x1, Pallas kernels, cross_block(): pl.pallas_call(cross_kernel, out_shape=jax.ShapeDtypeStruct((TOK, D), jnp...  9.48 us
    all_to_all x1, starting transfers between devices, local(): lax.all_to_all(packets, ('pairs', 'mp'), split_axis=0, concat_axis=0, til...  9.38 us
    pallas_call x1, Pallas kernels, self_block(): pl.pallas_call(self_kernel, out_shape=jax.ShapeDtypeStruct((TOK, D), jnp....  9.02 us
    ppermute x3, starting transfers between devices, from_mp(): lax.ppermute(value, 'mp', [((index + apart) % MP, index) for index in ran...  6.52 us
  transfers between devices with their start and end apart: 11, of which 9 were waited for; matrix products, arithmetic and copies ran while one was open for 0% of the time, Pallas kernels for 11%

profile of v5, /device:TPU:2, one launch (start us, length us, event | category | flops | bytes accessed | tf_op | source)
XLA Modules:
  0.0 132.5 jit_solution(1054954716824581946)
XLA Ops:
  6.5 0.0 copy-start
  6.5 0.0 all-gather.3.cloned.1.call-start
  6.5 2.3 %together.1 = bf16[5,192,768]{2,1,0:T(8,128)(2,1)} custom-call(bf16[3,192,768]{2,1,0:T(8,128)(2,1)} %bitcast.52, bf16[2,192,768]{2,1,0:T(8,128)(2,1)} %bitcast.53), custom_call_target="tpu_custom_call" | custom-call | bytes 2949120 | tf_op jit(solution)/shard_map/together/pallas_call | solution.py:323
  8.8 0.0 all-gather.3.cloned.1.call-update
  8.9 3.8 %embed.1 = bf16[32,4,8,384]{3,2,1,0:T(8,128)(2,1)} custom-call(s32[1]{0:T(128)} %bitcast.2.side_ref, bf16[8,128,1024]{2,1,0:T(8,128)(2,1)} %tokens_ref.1, bf16[1024,768]{1,0:T(8,128)(2,1)} %weight_ref.1), custom_call_target="tpu_custom_call" | custom-call | flops 805306368 | bytes 3407872 | tf_op jit(solution)/shard_map/embed/pallas_call | solution.py:72
  12.7 0.0 copy-start.10
  12.7 0.0 copy-start.11
  12.7 11.8 %all-to-all-start = ((bf16[32,4,8,384]{3,2,1,0:T(8,128)(2,1)}), bf16[32,4,8,384]{3,2,1,0:T(8,128)(2,1)S(1)}, u32[]{:S(2)}, u32[]{:S(2)}) async-start(bf16[32,4,8,384]{3,2,1,0:T(8,128)(2,1)} %embed.1), calls=%async_computation | async-start | bytes 1572864 | tf_op jit(solution)/shard_map/all_to_all | solution.py:359
  24.5 0.0 copy-done.10
  24.5 3.3 %collective-permute-start.1 = (bf16[48,768]{1,0:T(8,128)(2,1)S(1)}, bf16[48,768]{1,0:T(8,128)(2,1)S(1)}, u32[]{:S(2)}, u32[]{:S(2)}) collective-permute-start(bf16[48,768]{1,0:T(8,128)(2,1)S(1)} %dynamic-slice_bitcast_fusion), channel_id=1, source_target_pairs={{2,0},{3,1},{0,2},{1,3},{6,4},{7,5},{4,6},{5,7},{10,8},{11,9},{8,1... | collective-permute-start | bytes 221192 | tf_op jit(solution)/shard_map/ppermute | solution.py:294
  27.8 0.7 collective-permute-start.2
  28.4 2.6 %collective-permute-start = (bf16[48,768]{1,0:T(8,128)(2,1)S(1)}, bf16[48,768]{1,0:T(8,128)(2,1)S(1)}, u32[]{:S(2)}, u32[]{:S(2)}) collective-permute-start(bf16[48,768]{1,0:T(8,128)(2,1)S(1)} %dynamic-slice_bitcast_fusion), channel_id=1, source_target_pairs={{1,0},{2,1},{3,2},{0,3},{5,4},{6,5},{7,6},{4,7},{9,8},{10,9},{11,1... | collective-permute-start | bytes 221192 | tf_op jit(solution)/shard_map/ppermute | solution.py:294
  31.0 1.8 %collective-permute-done.1 = bf16[48,768]{1,0:T(8,128)(2,1)S(1)} collective-permute-done((bf16[48,768]{1,0:T(8,128)(2,1)S(1)}, bf16[48,768]{1,0:T(8,128)(2,1)S(1)}, u32[]{:S(2)}, u32[]{:S(2)}) %collective-permute-start.1) | collective-permute-done | bytes 73760 | tf_op jit(solution)/shard_map/ppermute | solution.py:294
  32.8 2.4 %collective-permute-done.2 = bf16[48,768]{1,0:T(8,128)(2,1)S(1)} collective-permute-done((bf16[48,768]{1,0:T(8,128)(2,1)S(1)}, bf16[48,768]{1,0:T(8,128)(2,1)S(1)}, u32[]{:S(2)}, u32[]{:S(2)}) %collective-permute-start.2) | collective-permute-done | bytes 73760 | tf_op jit(solution)/shard_map/ppermute | solution.py:294
  35.2 0.0 collective-permute-done
  35.2 0.1 select_bitcast_fusion.3
  35.3 11.6 %all-to-all-done = bf16[32,4,8,384]{3,2,1,0:T(8,128)(2,1)S(1)} async-done(((bf16[32,4,8,384]{3,2,1,0:T(8,128)(2,1)}), bf16[32,4,8,384]{3,2,1,0:T(8,128)(2,1)S(1)}, u32[]{:S(2)}, u32[]{:S(2)}) %all-to-all-start) | async-done | bytes 786464 | tf_op jit(solution)/shard_map/all_to_all | solution.py:359
  46.9 0.0 collective-permute-start.3
  46.9 0.0 copy-done.11
  46.9 0.0 copy-start.9
  46.9 2.2 %collective-permute-done.3.other_ref = bf16[128,8,384]{2,1,0:T(8,128)(2,1)S(1)} collective-permute-done((bf16[128,8,384]{2,1,0:T(8,128)(2,1)S(1)}, bf16[128,8,384]{2,1,0:T(8,128)(2,1)S(1)}, u32[]{:S(2)}, u32[]{:S(2)}) %collective-permute-start.3) | collective-permute-done | bytes 786464 | tf_op jit(solution)/shard_map/ppermute | solution.py:367
  49.2 1.8 %pick.1 = bf16[128,8,384]{2,1,0:T(8,128)(2,1)} custom-call(s32[128]{0:T(128)S(1)} %compare_select_fusion.slots_ref, bf16[128,8,384]{2,1,0:T(8,128)(2,1)S(1)} %bitcast.46, bf16[128,8,384]{2,1,0:T(8,128)(2,1)S(1)} %collective-permute-done.3.other_ref), custom_call_target="tpu_custom_call" | custom-call | flops 393216 | bytes 2359296 | tf_op jit(solution)/shard_map/pick/pallas_call | solution.py:103
  51.0 9.4 %all-to-all-start.1 = ((bf16[128,8,384]{2,1,0:T(8,128)(2,1)}), bf16[128,8,384]{2,1,0:T(8,128)(2,1)S(1)}, u32[]{:S(2)}, u32[]{:S(2)}) async-start(bf16[128,8,384]{2,1,0:T(8,128)(2,1)} %pick.1), calls=%async_computation.1 | async-start | bytes 1572864 | tf_op jit(solution)/shard_map/all_to_all | solution.py:373
  60.3 1.5 %collective-permute-start.6 = (bf16[4,48,768]{2,1,0:T(8,128)(2,1)S(1)}, bf16[4,48,768]{2,1,0:T(8,128)(2,1)S(1)}, u32[]{:S(2)}, u32[]{:S(2)}) collective-permute-start(bf16[4,48,768]{2,1,0:T(8,128)(2,1)S(1)} %pad_maximum_fusion.slices0_ref), channel_id=1, source_target_pairs={{24,0},{0,8},{8,16},{16,24},{56,32},{32,40},{40,48},{48,56},{88,64... | collective-permute-start | bytes 884744 | tf_op jit(solution)/shard_map/ppermute | solution.py:300
  61.9 1.5 %collective-permute-start.5 = (bf16[4,48,768]{2,1,0:T(8,128)(2,1)S(1)}, bf16[4,48,768]{2,1,0:T(8,128)(2,1)S(1)}, u32[]{:S(2)}, u32[]{:S(2)}) collective-permute-start(bf16[4,48,768]{2,1,0:T(8,128)(2,1)S(1)} %pad_maximum_fusion.slices0_ref), channel_id=1, source_target_pairs={{16,0},{24,8},{0,16},{8,24},{48,32},{56,40},{32,48},{40,56},{80,64... | collective-permute-start | bytes 884744 | tf_op jit(solution)/shard_map/ppermute | solution.py:300
  63.4 1.7 %collective-permute-start.4 = (bf16[4,48,768]{2,1,0:T(8,128)(2,1)S(1)}, bf16[4,48,768]{2,1,0:T(8,128)(2,1)S(1)}, u32[]{:S(2)}, u32[]{:S(2)}) collective-permute-start(bf16[4,48,768]{2,1,0:T(8,128)(2,1)S(1)} %pad_maximum_fusion.slices0_ref), channel_id=1, source_target_pairs={{8,0},{16,8},{24,16},{0,24},{40,32},{48,40},{56,48},{32,56},{72,64... | collective-permute-start | bytes 884744 | tf_op jit(solution)/shard_map/ppermute | solution.py:300
  65.1 10.3 %collective-permute-done.6.slices3_ref = bf16[4,48,768]{2,1,0:T(8,128)(2,1)S(1)} collective-permute-done((bf16[4,48,768]{2,1,0:T(8,128)(2,1)S(1)}, bf16[4,48,768]{2,1,0:T(8,128)(2,1)S(1)}, u32[]{:S(2)}, u32[]{:S(2)}) %collective-permute-start.6) | collective-permute-done | bytes 294944 | tf_op jit(solution)/shard_map/ppermute | solution.py:300
  75.4 0.0 copy-start.3
  75.4 0.7 copy-done.3
  76.1 2.8 %collective-permute-done.5.slices2_ref = bf16[4,48,768]{2,1,0:T(8,128)(2,1)S(1)} collective-permute-done((bf16[4,48,768]{2,1,0:T(8,128)(2,1)S(1)}, bf16[4,48,768]{2,1,0:T(8,128)(2,1)S(1)}, u32[]{:S(2)}, u32[]{:S(2)}) %collective-permute-start.5) | collective-permute-done | bytes 294944 | tf_op jit(solution)/shard_map/ppermute | solution.py:300
  79.0 0.7 copy-done.5
  79.7 5.1 %collective-permute-done.4.slices1_ref = bf16[4,48,768]{2,1,0:T(8,128)(2,1)S(1)} collective-permute-done((bf16[4,48,768]{2,1,0:T(8,128)(2,1)S(1)}, bf16[4,48,768]{2,1,0:T(8,128)(2,1)S(1)}, u32[]{:S(2)}, u32[]{:S(2)}) %collective-permute-start.4) | collective-permute-done | bytes 294944 | tf_op jit(solution)/shard_map/ppermute | solution.py:300
  84.8 0.7 copy-done.7
  85.5 0.7 all-to-all-done.1.pieces_ref
  86.2 0.0 collective-permute-start.7
  86.2 1.8 %all-gather.3.cloned.1.call-done = bf16[20,192,768]{2,1,0:T(8,128)(2,1)} async-done(((bf16[5,192,768]{2,1,0:T(8,128)(2,1)}), bf16[20,192,768]{2,1,0:T(8,128)(2,1)}) %all-gather.3.cloned.1.call-update) | async-done | bytes 5898256 | tf_op jit(solution)/shard_map/all_gather | solution.py:354
  88.0 0.0 copy-done.9
  88.0 1.3 copy-done.1
  89.2 9.0 %self_block.1.after_ref = f32[512,768]{1,0:T(8,128)S(1)} custom-call(bf16[128,8,384]{2,1,0:T(8,128)(2,1)S(1)} %all-to-all-done.1.pieces_ref, bf16[4,5,192,768]{3,2,1,0:T(8,128)(2,1)} %bitcast.54, bf16[768,768]{1,0:T(8,128)(2,1)S(1)} %bitcast.48, f32[4,768]{1,0:T(4,128)S(1)} %bitcast.50), custom_call_target="tpu_custom_call" | custom-call | flops 3221225472 | bytes 8388608 | tf_op jit(solution)/shard_map/self_block/pallas_call | solution.py:259
  98.3 0.0 collective-permute-done.7.pieces_ref
  98.3 0.0 copy-done.2
  98.3 0.0 copy-done.4
  98.3 0.0 copy-done.6
  98.3 0.0 copy-done.8
  98.3 9.5 %cross_block.1 = bf16[512,768]{1,0:T(8,128)(2,1)S(1)} custom-call(s32[1]{0:T(128)} %bitcast.place_ref, f32[512,768]{1,0:T(8,128)S(1)} %self_block.1.after_ref, bf16[128,8,384]{2,1,0:T(8,128)(2,1)S(1)} %collective-permute-done.7.pieces_ref, bf16[4,48,768]{2,1,0:T(8,128)(2,1)S(1)} %pad_maximum_fusion.slices0_ref, bf16[4,48,768]{2,1,0:T(8,128)(2,1)S(1)} %copy-done.8, ...), custom_call_target="tpu_custom_call" | custom-call | flops 3221225472 | bytes 8388608 | tf_op jit(solution)/shard_map/cross_block/pallas_call | solution.py:274
  107.8 15.9 %all_to_all.15 = bf16[4,128,768]{2,1,0:T(8,128)(2,1)S(1)} all-to-all(bf16[4,128,768]{2,1,0:T(8,128)(2,1)S(1)} %bitcast.47), channel_id=1, replica_groups=mesh['pairs'=32,'side'=2,'mp'=4] {'mp'}, dimensions={0} | all-to-all | bytes 1572864 | tf_op jit(solution)/shard_map/all_to_all | solution.py:379
  123.7 0.0 copy-done
  123.7 2.0 %fusion.5 = bf16[4,1,128,1024]{3,2,1,0:T(8,128)(2,1)} fusion(bf16[4,128,768]{2,1,0:T(8,128)(2,1)S(1)} %all_to_all.15, bf16[1,768,1024]{2,1,0:T(8,128)(2,1)S(1)} %copy-done), kind=kOutput, calls=%fused_computation.3 | convolution fusion | flops 805830656 | bytes 3407872 | tf_op jit(solution)/shard_map/prd,de->pre/dot_general | solution.py:382
  (10 shorter events, 0.1 us)
Async XLA Ops:
  6.5 117.2 %copy-start = (bf16[1,768,1024]{2,1,0:T(8,128)(2,1)S(1)}, bf16[1,768,1024]{2,1,0:T(8,128)(2,1)}, u32[]{:S(2)}) copy-start(bf16[1,768,1024]{2,1,0:T(8,128)(2,1)} %param.19) | copy-start | bytes 4718596
  6.5 81.4 %all-gather.3.cloned.1.call-start = ((), (), s32[]{:S(2)}) async-start(), calls=%async_computation.3 | async-start | bytes 7372800 | tf_op jit(solution)/shard_map/all_gather | solution.py:354
  12.7 11.8 %copy-start.10 = (bf16[1,768,192]{1,2,0:T(8,128)(2,1)S(1)}, bf16[1,768,192]{1,2,0:T(8,128)(2,1)}, u32[]{:S(2)}) copy-start(bf16[1,768,192]{1,2,0:T(8,128)(2,1)} %param.15) | copy-start | bytes 884740
  12.7 34.2 %copy-start.11 = (s32[128,2]{0,1:T(2,128)S(1)}, s32[128,2]{0,1:T(2,128)}, u32[]{:S(2)}) copy-start(s32[128,2]{0,1:T(2,128)} %param.11) | copy-start | bytes 3076
  12.7 34.2 %all-to-all-start = ((bf16[32,4,8,384]{3,2,1,0:T(8,128)(2,1)}), bf16[32,4,8,384]{3,2,1,0:T(8,128)(2,1)S(1)}, u32[]{:S(2)}, u32[]{:S(2)}) async-start(bf16[32,4,8,384]{3,2,1,0:T(8,128)(2,1)} %embed.1), calls=%async_computation | async-start | bytes 1572864 | tf_op jit(solution)/shard_map/all_to_all | solution.py:359
  24.5 8.3 %collective-permute-start.1 = (bf16[48,768]{1,0:T(8,128)(2,1)S(1)}, bf16[48,768]{1,0:T(8,128)(2,1)S(1)}, u32[]{:S(2)}, u32[]{:S(2)}) collective-permute-start(bf16[48,768]{1,0:T(8,128)(2,1)S(1)} %dynamic-slice_bitcast_fusion), channel_id=1, source_target_pairs={{2,0},{3,1},{0,2},{1,3},{6,4},{7,5},{4,6},{5,7},{10,8},{11,9},{8,1... | collective-permute-start | bytes 221192 | tf_op jit(solution)/shard_map/ppermute | solution.py:294
  27.8 7.4 %collective-permute-start.2 = (bf16[48,768]{1,0:T(8,128)(2,1)S(1)}, bf16[48,768]{1,0:T(8,128)(2,1)S(1)}, u32[]{:S(2)}, u32[]{:S(2)}) collective-permute-start(bf16[48,768]{1,0:T(8,128)(2,1)S(1)} %dynamic-slice_bitcast_fusion), channel_id=1, source_target_pairs={{3,0},{0,1},{1,2},{2,3},{7,4},{4,5},{5,6},{6,7},{11,8},{8,9},{9,10... | collective-permute-start | bytes 221192 | tf_op jit(solution)/shard_map/ppermute | solution.py:294
  28.4 6.7 %collective-permute-start = (bf16[48,768]{1,0:T(8,128)(2,1)S(1)}, bf16[48,768]{1,0:T(8,128)(2,1)S(1)}, u32[]{:S(2)}, u32[]{:S(2)}) collective-permute-start(bf16[48,768]{1,0:T(8,128)(2,1)S(1)} %dynamic-slice_bitcast_fusion), channel_id=1, source_target_pairs={{1,0},{2,1},{3,2},{0,3},{5,4},{6,5},{7,6},{4,7},{9,8},{10,9},{11,1... | collective-permute-start | bytes 221192 | tf_op jit(solution)/shard_map/ppermute | solution.py:294
  46.9 2.3 %collective-permute-start.3 = (bf16[128,8,384]{2,1,0:T(8,128)(2,1)S(1)}, bf16[128,8,384]{2,1,0:T(8,128)(2,1)S(1)}, u32[]{:S(2)}, u32[]{:S(2)}) collective-permute-start(bf16[128,8,384]{2,1,0:T(8,128)(2,1)S(1)} %bitcast.45), channel_id=1, source_target_pairs={{0,4},{4,0},{1,5},{5,1},{2,6},{6,2},{3,7},{7,3},{8,12},{12,8},{9,1... | collective-permute-start | bytes 2359304 | tf_op jit(solution)/shard_map/ppermute | solution.py:367
  46.9 41.0 %copy-start.9 = (f32[1,4,768]{2,1,0:T(4,128)S(1)}, f32[1,4,768]{2,1,0:T(4,128)}, u32[]{:S(2)}) copy-start(f32[1,4,768]{2,1,0:T(4,128)} %param.18) | copy-start | bytes 36868
  51.0 35.2 %all-to-all-start.1 = ((bf16[128,8,384]{2,1,0:T(8,128)(2,1)}), bf16[128,8,384]{2,1,0:T(8,128)(2,1)S(1)}, u32[]{:S(2)}, u32[]{:S(2)}) async-start(bf16[128,8,384]{2,1,0:T(8,128)(2,1)} %pick.1), calls=%async_computation.1 | async-start | bytes 1572864 | tf_op jit(solution)/shard_map/all_to_all | solution.py:373
  60.3 15.1 %collective-permute-start.6 = (bf16[4,48,768]{2,1,0:T(8,128)(2,1)S(1)}, bf16[4,48,768]{2,1,0:T(8,128)(2,1)S(1)}, u32[]{:S(2)}, u32[]{:S(2)}) collective-permute-start(bf16[4,48,768]{2,1,0:T(8,128)(2,1)S(1)} %pad_maximum_fusion.slices0_ref), channel_id=1, source_target_pairs={{24,0},{0,8},{8,16},{16,24},{56,32},{32,40},{40,48},{48,56},{88,64... | collective-permute-start | bytes 884744 | tf_op jit(solution)/shard_map/ppermute | solution.py:300
  61.9 17.1 %collective-permute-start.5 = (bf16[4,48,768]{2,1,0:T(8,128)(2,1)S(1)}, bf16[4,48,768]{2,1,0:T(8,128)(2,1)S(1)}, u32[]{:S(2)}, u32[]{:S(2)}) collective-permute-start(bf16[4,48,768]{2,1,0:T(8,128)(2,1)S(1)} %pad_maximum_fusion.slices0_ref), channel_id=1, source_target_pairs={{16,0},{24,8},{0,16},{8,24},{48,32},{56,40},{32,48},{40,56},{80,64... | collective-permute-start | bytes 884744 | tf_op jit(solution)/shard_map/ppermute | solution.py:300
  63.4 21.4 %collective-permute-start.4 = (bf16[4,48,768]{2,1,0:T(8,128)(2,1)S(1)}, bf16[4,48,768]{2,1,0:T(8,128)(2,1)S(1)}, u32[]{:S(2)}, u32[]{:S(2)}) collective-permute-start(bf16[4,48,768]{2,1,0:T(8,128)(2,1)S(1)} %pad_maximum_fusion.slices0_ref), channel_id=1, source_target_pairs={{8,0},{16,8},{24,16},{0,24},{40,32},{48,40},{56,48},{32,56},{72,64... | collective-permute-start | bytes 884744 | tf_op jit(solution)/shard_map/ppermute | solution.py:300
  75.4 0.7 copy-start.3
  79.0 0.7 copy-start.5
  84.8 0.7 copy-start.7
  86.2 12.1 %collective-permute-start.7 = (bf16[128,8,384]{2,1,0:T(8,128)(2,1)S(1)}, bf16[128,8,384]{2,1,0:T(8,128)(2,1)S(1)}, u32[]{:S(2)}, u32[]{:S(2)}) collective-permute-start(bf16[128,8,384]{2,1,0:T(8,128)(2,1)S(1)} %all-to-all-done.1.pieces_ref), channel_id=1, source_target_pairs={{0,4},{4,0},{1,5},{5,1},{2,6},{6,2},{3,7},{7,3},{8,12},{12,8},{9,1... | collective-permute-start | bytes 2359304 | tf_op jit(solution)/shard_map/ppermute | solution.py:375
  88.0 1.3 copy-start.1
  89.2 9.1 %copy-start.2 = (bf16[1,768,768]{2,1,0:T(8,128)(2,1)S(1)}, bf16[1,768,768]{2,1,0:T(8,128)(2,1)}, u32[]{:S(2)}) copy-start(bf16[1,768,768]{2,1,0:T(8,128)(2,1)} %param.17) | copy-start | bytes 3538948
  89.2 9.1 %copy-start.4 = (bf16[4,48,768]{2,1,0:T(8,128)(2,1)S(1)}, bf16[4,48,768]{2,1,0:T(8,128)(2,1)}, u32[]{:S(2)}) copy-start(bf16[4,48,768]{2,1,0:T(8,128)(2,1)} %copy-done.3) | copy-start | bytes 884740
  89.2 9.1 %copy-start.6 = (bf16[4,48,768]{2,1,0:T(8,128)(2,1)S(1)}, bf16[4,48,768]{2,1,0:T(8,128)(2,1)}, u32[]{:S(2)}) copy-start(bf16[4,48,768]{2,1,0:T(8,128)(2,1)} %copy-done.5) | copy-start | bytes 884740
  89.2 9.1 %copy-start.8 = (bf16[4,48,768]{2,1,0:T(8,128)(2,1)S(1)}, bf16[4,48,768]{2,1,0:T(8,128)(2,1)}, u32[]{:S(2)}) copy-start(bf16[4,48,768]{2,1,0:T(8,128)(2,1)} %copy-done.7) | copy-start | bytes 884740
Sparse Core Ops, SparseCore 0:
  9.2 78.7 all-gather.2
